TPU v7x, 32 devices: a whole 2x2x4 slice. The times are simulated.
32 devices in a mesh: group: 2 (over y), along: 8 (over z, x), cross: 2 (over core).
Axes of the slice: x: 2, y: 2, z: 4, core: 2. Of those that a mesh axis runs over, the one named last changes fastest.
Arguments:
- floc_conc: float32 [15, 8, 64, 512], P(None, None, ('group', 'along'), 'cross'), parts along dimension 2, may hold values from 0.05 to 2
- currents: float32 [2, 64, 512], P(None, ('group', 'along'), 'cross'), parts along dimension 1, may hold values from -0.3 to 0.3
- water_depth: float32 [64, 512], P(('group', 'along'), 'cross'), parts along dimension 0, may hold values from 0.5 to 8
- wet_mask: int32 [64, 512], P(('group', 'along'), 'cross'), parts along dimension 0, may hold values 0 or 1
- shear_rate: float32 [8, 64, 512], P(None, ('group', 'along'), 'cross'), parts along dimension 1, may hold values from 0.1 to 1
- aggregation: float32 [15, 15], replicated, may hold values from -1.5 to 1.5
- breakup: float32 [15, 15], replicated, may hold values from -1.5 to 1.5
- settling: float32 [15], replicated, may hold values from 0.05 to 0.4
- erosion: float32 [15], replicated, may hold values from 0.05 to 0.5
- action_density: float32 [36, 16, 32, 256], P(None, None, ('group', 'along', 'cross')), parts along dimension 2, may hold values from 0.1 to 2
- wind_growth: float32 [36, 16], replicated, may hold values from -0.3 to 0.3
Outputs:
- floc_next: float32 [15, 8, 64, 512], P(None, None, ('group', 'along'), 'cross'), parts along dimension 2
- action_next: float32 [36, 16, 32, 256], P(None, None, ('group', 'along', 'cross')), parts along dimension 2
There are 2 independent parts, one for each index of `group`. A program takes and returns all parts, laid end to end along the dimension named above; an argument that names none is the same for every part. Nothing has to cross between parts.
Inputs may be any that keep to these rules, and one draw needn't show every extreme that they name: `wet_mask`: 1 marks a wet ocean cell, 0 a dry one.
All inputs are finite; a program needn't handle non-finite values. No bound on the sum of `wet_mask` on one device may be relied on, other than what follows from the above.
Results may differ from a plain program's by a relative error of at most 0.00017.
Values sent between devices are 32-bit elements; how exact they have to be, the bound alone decides.
A program may use at most 64 MiB of HBM per device.

v0:
```python
import math

import jax
import jax.numpy as jnp
from jax import lax
from jax.sharding import PartitionSpec as P

SUBSTEPS = 4


diffusion_rate = 0.05
threshold_stress = 0.25


def padded_2(shard, sides, width):
    for axis, dim in sides:
        peers, length = (lax.axis_size(axis), shard.shape[dim])
        up = [(i, (i + 1) % peers) for i in range(peers - 1)]
        down = [(j, i) for i, j in up]
        last = lax.slice_in_dim(shard, length - width, length, axis=dim)
        initial = lax.slice_in_dim(shard, 0, width, axis=dim)
        before = lax.ppermute(last, axis, up)
        after = lax.ppermute(initial, axis, down)
        shard = jnp.concatenate([before, shard, after], axis=dim)
    return shard


def coarsen(field):
    row_count, col_count = field.shape
    blocks = field.reshape(row_count // 2, 2, col_count // 2, 2)
    return jnp.sum(blocks, axis=(1, 3)) * 0.25


def shoaling(depth_coarse, freq_count):
    factors = (1.0 + 3.0 * jnp.arange(freq_count).astype(jnp.float32) / freq_count) * 0.25
    return jnp.tanh(depth_coarse[None] * factors[:, None, None])


def stress_excess(eastward, northward, orbital_tile, wet_float):
    orbital_fine = jnp.repeat(jnp.repeat(orbital_tile, 2, axis=0), 2, axis=1)
    stress = 0.5 * (eastward * eastward + northward * northward) + orbital_fine
    return wet_float * jnp.maximum(stress - threshold_stress, 0.0)


def advance(
    padded, east_padded, north_padded, shear_rate, excess, aggregation, breakup, settling, erosion
):
    centre = padded[:, :, 1:-1, 1:-1]
    eastward = east_padded[1:-1, 1:-1]
    northward = north_padded[1:-1, 1:-1]
    give_east = jnp.maximum(east_padded, 0.0) + diffusion_rate
    give_west = jnp.maximum(-east_padded, 0.0) + diffusion_rate
    give_north = jnp.maximum(north_padded, 0.0) + diffusion_rate
    give_south = jnp.maximum(-north_padded, 0.0) + diffusion_rate
    leaving = jnp.abs(eastward) + jnp.abs(northward) + 4.0 * diffusion_rate
    moved_conc = centre - leaving * centre
    moved_conc = moved_conc + give_east[:-2, 1:-1] * padded[:, :, :-2, 1:-1]
    moved_conc = moved_conc + give_west[2:, 1:-1] * padded[:, :, 2:, 1:-1]
    moved_conc = moved_conc + give_north[1:-1, :-2] * padded[:, :, 1:-1, :-2]
    moved_conc = moved_conc + give_south[1:-1, 2:] * padded[:, :, 1:-1, 2:]
    mixed_conc = jnp.einsum(
        "kc,clxy->klxy", aggregation, moved_conc, precision=lax.Precision.HIGHEST
    )
    broken_up = jnp.einsum("kc,clxy->klxy", breakup, moved_conc, precision=lax.Precision.HIGHEST)
    reacted = moved_conc + 0.25 * shear_rate[None] * moved_conc * mixed_conc + 0.25 * broken_up
    settle_rate = settling[:, None, None, None]
    from_above = jnp.concatenate([reacted[:, 1:], jnp.zeros_like(reacted[:, :1])], axis=1)
    settled = reacted - settle_rate * reacted + settle_rate * from_above
    lifted = erosion[:, None, None] * excess[None]
    return settled.at[:, 0].add(lifted)


def wave_speeds(shoaling_factor, wet_coarse, dir_count):
    angles = (jnp.arange(dir_count).astype(jnp.float32) + 0.5) * (
        2.0 * math.pi / dir_count
    ) - 0.5 * math.pi
    group_speed = 0.45 * shoaling_factor * wet_coarse[None]
    speed_x = jnp.cos(angles)[:, None, None, None] * group_speed[None]
    speed_y = jnp.sin(angles)[:, None, None, None] * group_speed[None]
    return (speed_x, speed_y)


def finish_waves(action_density, flux_x, inflow_x, speed_y, shoaling_factor, wind_growth):
    give_north = jnp.maximum(speed_y, 0.0) * action_density
    give_south = jnp.maximum(-speed_y, 0.0) * action_density
    zeros_edge = jnp.zeros_like(action_density[..., :1])
    inflow_y = jnp.concatenate([zeros_edge, give_north[..., :-1]], axis=-1) + jnp.concatenate(
        [give_south[..., 1:], zeros_edge], axis=-1
    )
    propagated = action_density - flux_x - (give_north + give_south) + inflow_x + inflow_y
    turning = 0.2 * (1.0 - shoaling_factor)[None]
    spread = propagated + turning * (
        jnp.roll(propagated, 1, axis=0) + jnp.roll(propagated, -1, axis=0) - 2.0 * propagated
    )
    energy = jnp.mean(spread, axis=(0, 1))
    return spread * jnp.exp(wind_growth[:, :, None, None] - 0.5 * energy[None, None])


def with_rims(stacked, width):
    return padded_2(stacked, (("along", 1), ("cross", 2)), width)


def body(
    floc_conc,
    currents,
    water_depth,
    wet_mask,
    shear_rate,
    aggregation,
    breakup,
    settling,
    erosion,
    action_density,
    wind_growth,
):
    class_count, level_count, row_count, col_count = floc_conc.shape
    layer_count = class_count * level_count
    dir_count, freq_count = wind_growth.shape
    wet_float = wet_mask.astype(jnp.float32)
    eastward = currents[0] * wet_float
    northward = currents[1] * wet_float
    ocean_tile = jnp.stack([coarsen(water_depth), coarsen(wet_float)])
    ocean_strip = lax.all_to_all(ocean_tile, "cross", split_axis=1, concat_axis=2, tiled=True)
    depth_strip = ocean_strip[0]
    wet_strip = ocean_strip[1]
    shoaling_factor = shoaling(depth_strip, freq_count)
    orbital = wet_strip * jnp.mean(
        action_density * (1.0 - shoaling_factor * shoaling_factor)[None], axis=(0, 1)
    )
    orbital_tile = lax.all_to_all(orbital, "cross", split_axis=1, concat_axis=0, tiled=True)
    excess = stress_excess(eastward, northward, orbital_tile, wet_float)
    floc_state = floc_conc
    currents_masked = jnp.stack([eastward, northward])
    for substep in range(SUBSTEPS):
        stacked = jnp.concatenate(
            [floc_state.reshape(layer_count, row_count, col_count), currents_masked], axis=0
        )
        padded = with_rims(stacked, 1)
        layers = padded[:layer_count].reshape(
            class_count, level_count, row_count + 2, col_count + 2
        )
        floc_state = advance(
            layers,
            padded[layer_count],
            padded[layer_count + 1],
            shear_rate,
            excess,
            aggregation,
            breakup,
            settling,
            erosion,
        )
    speed_x, speed_y = wave_speeds(shoaling_factor, wet_strip, dir_count)
    flux_x = jnp.abs(speed_x) * action_density
    halfway = dir_count // 2
    padded_flux = padded_2(flux_x, ((("along", "cross"), 2),), 1)
    inflow_x = jnp.concatenate(
        [padded_flux[:halfway, :, :-2], padded_flux[halfway:, :, 2:]], axis=0
    )
    action_next = finish_waves(
        action_density, flux_x, inflow_x, speed_y, shoaling_factor, wind_growth
    )
    return (floc_state, action_next)


def solution(mesh):
    placed = (
        P(None, None, ("group", "along"), "cross"),
        P(None, ("group", "along"), "cross"),
        P(("group", "along"), "cross"),
        P(("group", "along"), "cross"),
        P(None, ("group", "along"), "cross"),
        P(),
        P(),
        P(),
        P(),
        P(None, None, ("group", "along", "cross"), None),
        P(),
    )
    return jax.shard_map(
        body,
        mesh=mesh,
        in_specs=placed,
        out_specs=(
            P(None, None, ("group", "along"), "cross"),
            P(None, None, ("group", "along", "cross"), None),
        ),
        check_vma=False,
    )
```

profile of v0, /device:TPU:0, one launch (start us, length us, event | category | flops | bytes accessed | tf_op | source)
XLA Modules:
  0.0 130.6 jit_solution(4908698115987739712)
XLA Ops:
  3.4 3.2 %all-to-all-start = ((f32[2,2,128]{2,0,1:T(2,128)}), f32[2,2,128]{2,0,1:T(2,128)S(1)}, u32[]{:S(2)}, u32[]{:S(2)}) async-start(f32[2,2,128]{2,0,1:T(2,128)} %pad_maximum_fusion.25), calls=%async_computation | async-start | bytes 4096 | tf_op jit(solution)/shard_map/all_to_all | solution.py:123
  6.7 1.3 all-to-all-done
  8.1 2.2 %fusion.34 = (f32[36,16,1,256]{3,2,1,0:T(1,128)S(1)}, f32[36,16,1,256]{3,2,1,0:T(1,128)S(1)}, f32[36,16,1,256]{3,2,1,0:T(1,128)S(1)}) fusion(f32[36,16,1,256]{3,2,1,0:T(1,128)S(1)} %copy-done.1, f32[16,256]{1,0:T(8,128)S(1)} %get-tuple-element.139, f32[36]{0:T(128)S(1)} %get-tuple-element.141, f32[36]{0:T(128)S(1)} %get-tuple-element.142), kind=kLoop, calls=%fused_computation.73 | loop fusion | flops 1327104 | bytes 2375968 | tf_op jit(solution)/shard_map/mul | solution.py:84
  10.3 2.1 %collective-permute-start.16 = (f32[36,16,1,256]{3,2,1,0:T(1,128)S(1)}, f32[36,16,1,256]{3,2,1,0:T(1,128)S(1)}, u32[]{:S(2)}, u32[]{:S(2)}) collective-permute-start(f32[36,16,1,256]{3,2,1,0:T(1,128)S(1)} %get-tuple-element.98), channel_id=1, source_target_pairs={{0,1},{1,2},{2,3},{3,4},{4,5},{5,6},{6,7},{7,8},{8,9},{9,10},{10,1... | collective-permute-start | bytes 1769480 | tf_op jit(solution)/shard_map/ppermute | solution.py:22
  12.4 1.3 collective-permute-start.17
  13.8 1.3 slice.552
  15.3 3.3 %collective-permute-done.17 = f32[36,16,1,256]{3,2,1,0:T(1,128)S(1)} collective-permute-done((f32[36,16,1,256]{3,2,1,0:T(1,128)S(1)}, f32[36,16,1,256]{3,2,1,0:T(1,128)S(1)}, u32[]{:S(2)}, u32[]{:S(2)}) %collective-permute-start.17) | collective-permute-done | bytes 589856 | tf_op jit(solution)/shard_map/ppermute | solution.py:23
  18.9 4.6 %fusion.37 = (f32[36,16,1,256]{3,2,1,0:T(1,128)S(1)}, f32[256]{0:T(256)S(1)}) fusion(f32[18,16,1,256]{3,2,1,0:T(1,128)S(1)} %slice.550, f32[18,16,1,256]{3,2,1,0:T(1,128)S(1)} %slice.549, f32[36,16,1,255]{3,2,1,0:T(1,128)S(1)} %slice.552, f32[36,16,1,255]{3,2,1,0:T(1,128)S(1)} %bitcast.158, f32[36,16,1,256]{3,2,1,0:T(1,128)S(1)} %copy-done.1, ...), kind=kLoop, calls=%fused_computation.77 | loop fusion | flops 2653952 | bytes 2978592 | tf_op jit(solution)/shard_map/add | solution.py:90
  23.5 13.1 %all_to_all.22 = f32[1,2,128]{2,0,1:T(1,128)S(1)} all-to-all(f32[1,2,128]{2,0,1:T(1,128)S(1)} %bitcast.168), channel_id=1, replica_groups=mesh['group'=2,'along'=8,'cross'=2] {'cross'}, dimensions={1} | all-to-all | bytes 2048 | tf_op jit(solution)/shard_map/all_to_all | solution.py:130
  36.9 4.8 %collective-permute-start = (f32[122,1,256]{2,0,1:T(8,128)S(1)}, f32[122,1,256]{2,0,1:T(8,128)S(1)}, u32[]{:S(2)}, u32[]{:S(2)}) collective-permute-start(f32[122,1,256]{2,0,1:T(8,128)S(1)} %get-tuple-element.111), channel_id=1, source_target_pairs={{0,2},{2,4},{4,6},{6,8},{8,10},{10,12},{12,14},{1,3},{3,5},{5,7},{... | collective-permute-start | bytes 374792 | tf_op jit(solution)/shard_map/ppermute | solution.py:22
  41.7 1.3 collective-permute-start.1
  43.0 1.8 %collective-permute-done = f32[122,1,256]{2,0,1:T(8,128)S(1)} collective-permute-done((f32[122,1,256]{2,0,1:T(8,128)S(1)}, f32[122,1,256]{2,0,1:T(8,128)S(1)}, u32[]{:S(2)}, u32[]{:S(2)}) %collective-permute-start) | collective-permute-done | bytes 124960 | tf_op jit(solution)/shard_map/ppermute | solution.py:22
  44.8 4.1 %collective-permute-done.1 = f32[122,1,256]{2,0,1:T(8,128)S(1)} collective-permute-done((f32[122,1,256]{2,0,1:T(8,128)S(1)}, f32[122,1,256]{2,0,1:T(8,128)S(1)}, u32[]{:S(2)}, u32[]{:S(2)}) %collective-permute-start.1) | collective-permute-done | bytes 124960 | tf_op jit(solution)/shard_map/ppermute | solution.py:23
  49.2 1.3 %collective-permute-start.2 = (f32[122,6,1]{2,0,1:T(8,128)S(1)}, f32[122,6,1]{2,0,1:T(8,128)S(1)}, u32[]{:S(2)}, u32[]{:S(2)}) collective-permute-start(f32[122,6,1]{2,0,1:T(8,128)S(1)} %get-tuple-element.94), channel_id=1, source_target_pairs={{0,1},{2,3},{4,5},{6,7},{8,9},{10,11},{12,13},{14,15},{16,17},{18,... | collective-permute-start | bytes 8792 | tf_op jit(solution)/shard_map/ppermute | solution.py:22
  50.5 1.3 collective-permute-start.3
  51.8 2.3 %collective-permute-done.3 = f32[122,6,1]{2,0,1:T(8,128)S(1)} collective-permute-done((f32[122,6,1]{2,0,1:T(8,128)S(1)}, f32[122,6,1]{2,0,1:T(8,128)S(1)}, u32[]{:S(2)}, u32[]{:S(2)}) %collective-permute-start.3) | collective-permute-done | bytes 2960 | tf_op jit(solution)/shard_map/ppermute | solution.py:23
  59.1 4.3 %collective-permute-start.4 = (f32[122,1,256]{2,1,0:T(1,128)S(1)}, f32[122,1,256]{2,1,0:T(1,128)S(1)}, u32[]{:S(2)}, u32[]{:S(2)}) collective-permute-start(f32[122,1,256]{2,1,0:T(1,128)S(1)} %get-tuple-element.109), channel_id=1, source_target_pairs={{0,2},{2,4},{4,6},{6,8},{8,10},{10,12},{12,14},{1,3},{3,5},{5,7},{... | collective-permute-start | bytes 374792 | tf_op jit(solution)/shard_map/ppermute | solution.py:22
  63.5 1.5 %collective-permute-start.5 = (f32[122,1,256]{2,1,0:T(1,128)S(1)}, f32[122,1,256]{2,1,0:T(1,128)S(1)}, u32[]{:S(2)}, u32[]{:S(2)}) collective-permute-start(f32[122,1,256]{2,1,0:T(1,128)S(1)} %get-tuple-element.110), channel_id=1, source_target_pairs={{2,0},{4,2},{6,4},{8,6},{10,8},{12,10},{14,12},{3,1},{5,3},{7,5},{... | collective-permute-start | bytes 374792 | tf_op jit(solution)/shard_map/ppermute | solution.py:23
  65.0 1.3 %collective-permute-done.4 = f32[122,1,256]{2,1,0:T(1,128)S(1)} collective-permute-done((f32[122,1,256]{2,1,0:T(1,128)S(1)}, f32[122,1,256]{2,1,0:T(1,128)S(1)}, u32[]{:S(2)}, u32[]{:S(2)}) %collective-permute-start.4) | collective-permute-done | bytes 124960 | tf_op jit(solution)/shard_map/ppermute | solution.py:22
  66.4 4.1 %collective-permute-done.5 = f32[122,1,256]{2,1,0:T(1,128)S(1)} collective-permute-done((f32[122,1,256]{2,1,0:T(1,128)S(1)}, f32[122,1,256]{2,1,0:T(1,128)S(1)}, u32[]{:S(2)}, u32[]{:S(2)}) %collective-permute-start.5) | collective-permute-done | bytes 124960 | tf_op jit(solution)/shard_map/ppermute | solution.py:23
  71.0 1.3 %collective-permute-start.6 = (f32[122,6,1]{2,1,0:T(8,128)S(1)}, f32[122,6,1]{2,1,0:T(8,128)S(1)}, u32[]{:S(2)}, u32[]{:S(2)}) collective-permute-start(f32[122,6,1]{2,1,0:T(8,128)S(1)} %get-tuple-element.92), channel_id=1, source_target_pairs={{0,1},{2,3},{4,5},{6,7},{8,9},{10,11},{12,13},{14,15},{16,17},{18,... | collective-permute-start | bytes 8792 | tf_op jit(solution)/shard_map/ppermute | solution.py:22
  72.3 1.3 collective-permute-start.7
  73.6 1.1 fusion.118
  74.8 1.3 %collective-permute-done.7 = f32[122,6,1]{2,1,0:T(8,128)S(1)} collective-permute-done((f32[122,6,1]{2,1,0:T(8,128)S(1)}, f32[122,6,1]{2,1,0:T(8,128)S(1)}, u32[]{:S(2)}, u32[]{:S(2)}) %collective-permute-start.7) | collective-permute-done | bytes 2960 | tf_op jit(solution)/shard_map/ppermute | solution.py:23
  76.1 1.5 %fusion.3 = f32[122,6,258]{2,1,0:T(8,128)S(1)} fusion(f32[1,4,256]{2,1,0:T(4,128)S(1)} %get-tuple-element.129, f32[1,4,256]{2,1,0:T(4,128)S(1)} %get-tuple-element.130, f32[122,6,1]{2,1,0:T(8,128)S(1)} %collective-permute-done.7, f32[122,1,256]{2,1,0:T(1,128)S(1)} %collective-permute-done.5, f32[120,4,256]{2,1,0:T(4,128)S(1)} %copy.103, ...), kind=kLoop, calls=%fused_computation.15 | loop fusion | flops 1133136 | bytes 1510848 | tf_op jit(solution)/shard_map/concatenate | solution.py:24
  77.7 1.1 fusion.111
  78.9 1.7 %fusion.47 = f32[15,8,4,256]{3,0,2,1:T(8,128)S(1)} fusion(f32[15,8,4,256]{3,2,1,0:T(4,128)S(1)} %get-tuple-element.82, f32[15,8,4,256]{3,2,1,0:T(4,128)S(1)} %get-tuple-element.79, f32[15,8,4,256]{3,2,1,0:T(4,128)S(1)} %get-tuple-element.80, f32[15,8,4,256]{3,2,1,0:T(4,128)S(1)} %get-tuple-element.81, f32[15,8,4,256]{3,2,1,0:T(4,128)S(1)} %get-tuple-element.78, ...), kind=kLoop, calls=%fused_computation.92 | loop fusion | flops 1228800 | bytes 2969600 | tf_op jit(solution)/shard_map/add | solution.py:60
  83.0 4.2 %collective-permute-start.8 = (f32[122,1,256]{2,1,0:T(1,128)S(1)}, f32[122,1,256]{2,1,0:T(1,128)S(1)}, u32[]{:S(2)}, u32[]{:S(2)}) collective-permute-start(f32[122,1,256]{2,1,0:T(1,128)S(1)} %get-tuple-element.107), channel_id=1, source_target_pairs={{0,2},{2,4},{4,6},{6,8},{8,10},{10,12},{12,14},{1,3},{3,5},{5,7},{... | collective-permute-start | bytes 374792 | tf_op jit(solution)/shard_map/ppermute | solution.py:22
  87.2 1.3 collective-permute-start.9
  88.5 1.6 %collective-permute-done.8 = f32[122,1,256]{2,1,0:T(1,128)S(1)} collective-permute-done((f32[122,1,256]{2,1,0:T(1,128)S(1)}, f32[122,1,256]{2,1,0:T(1,128)S(1)}, u32[]{:S(2)}, u32[]{:S(2)}) %collective-permute-start.8) | collective-permute-done | bytes 124960 | tf_op jit(solution)/shard_map/ppermute | solution.py:22
  90.1 4.1 %collective-permute-done.9 = f32[122,1,256]{2,1,0:T(1,128)S(1)} collective-permute-done((f32[122,1,256]{2,1,0:T(1,128)S(1)}, f32[122,1,256]{2,1,0:T(1,128)S(1)}, u32[]{:S(2)}, u32[]{:S(2)}) %collective-permute-start.9) | collective-permute-done | bytes 124960 | tf_op jit(solution)/shard_map/ppermute | solution.py:23
  94.8 1.3 %collective-permute-start.10 = (f32[122,6,1]{2,1,0:T(8,128)S(1)}, f32[122,6,1]{2,1,0:T(8,128)S(1)}, u32[]{:S(2)}, u32[]{:S(2)}) collective-permute-start(f32[122,6,1]{2,1,0:T(8,128)S(1)} %get-tuple-element.90), channel_id=1, source_target_pairs={{0,1},{2,3},{4,5},{6,7},{8,9},{10,11},{12,13},{14,15},{16,17},{18,... | collective-permute-start | bytes 8792 | tf_op jit(solution)/shard_map/ppermute | solution.py:22
  96.1 1.5 %collective-permute-start.11 = (f32[122,6,1]{2,1,0:T(8,128)S(1)}, f32[122,6,1]{2,1,0:T(8,128)S(1)}, u32[]{:S(2)}, u32[]{:S(2)}) collective-permute-start(f32[122,6,1]{2,1,0:T(8,128)S(1)} %get-tuple-element.91), channel_id=1, source_target_pairs={{1,0},{3,2},{5,4},{7,6},{9,8},{11,10},{13,12},{15,14},{17,16},{19,... | collective-permute-start | bytes 8792 | tf_op jit(solution)/shard_map/ppermute | solution.py:23
  97.6 1.7 %fusion.108 = (f32[256]{0:T(256)S(1)}, f32[36,16,1,256]{3,2,1,0:T(1,128)S(1)}) fusion(f32[36,16,1,256]{3,2,1,0:T(1,128)S(1)} %get-tuple-element.103, f32[1,16,1,256]{3,2,1,0:T(1,128)S(1)} %get-tuple-element.100, f32[35,16,1,256]{3,2,1,0:T(1,128)S(1)} %get-tuple-element.102, f32[35,16,1,256]{3,2,1,0:T(1,128)S(1)} %get-tuple-element.101, ...), kind=kLoop, calls=%fused_computation.229 | loop fusion | flops 1179392 | bytes 2376704 | tf_op jit(solution)/shard_map/reduce_sum | solution.py:95
  99.9 1.5 %fusion.7 = f32[122,6,258]{2,1,0:T(8,128)S(1)} fusion(f32[1,4,256]{2,1,0:T(4,128)S(1)} %get-tuple-element.129, f32[1,4,256]{2,1,0:T(4,128)S(1)} %get-tuple-element.130, f32[122,6,1]{2,1,0:T(8,128)S(1)} %collective-permute-done.11, f32[122,1,256]{2,1,0:T(1,128)S(1)} %collective-permute-done.9, f32[120,4,256]{2,1,0:T(4,128)S(1)} %copy.111, ...), kind=kLoop, calls=%fused_computation.19 | loop fusion | flops 1133136 | bytes 1510848 | tf_op jit(solution)/shard_map/concatenate | solution.py:24
  101.5 1.1 fusion.110
  102.7 1.4 %fusion.52 = f32[15,8,4,256]{3,0,2,1:T(8,128)S(1)} fusion(f32[15,8,4,256]{3,2,1,0:T(4,128)S(1)} %get-tuple-element.77, f32[15,8,4,256]{3,2,1,0:T(4,128)S(1)} %get-tuple-element.74, f32[15,8,4,256]{3,2,1,0:T(4,128)S(1)} %get-tuple-element.75, f32[15,8,4,256]{3,2,1,0:T(4,128)S(1)} %get-tuple-element.76, f32[15,8,4,256]{3,2,1,0:T(4,128)S(1)} %get-tuple-element.73, ...), kind=kLoop, calls=%fused_computation.97 | loop fusion | flops 1228800 | bytes 2969600 | tf_op jit(solution)/shard_map/add | solution.py:60
  106.4 3.8 %collective-permute-start.12 = (f32[122,1,256]{2,1,0:T(1,128)S(1)}, f32[122,1,256]{2,1,0:T(1,128)S(1)}, u32[]{:S(2)}, u32[]{:S(2)}) collective-permute-start(f32[122,1,256]{2,1,0:T(1,128)S(1)} %get-tuple-element.105), channel_id=1, source_target_pairs={{0,2},{2,4},{4,6},{6,8},{8,10},{10,12},{12,14},{1,3},{3,5},{5,7},{... | collective-permute-start | bytes 374792 | tf_op jit(solution)/shard_map/ppermute | solution.py:22
  110.3 1.3 collective-permute-start.13
  111.6 2.1 %collective-permute-done.12 = f32[122,1,256]{2,1,0:T(1,128)S(1)} collective-permute-done((f32[122,1,256]{2,1,0:T(1,128)S(1)}, f32[122,1,256]{2,1,0:T(1,128)S(1)}, u32[]{:S(2)}, u32[]{:S(2)}) %collective-permute-start.12) | collective-permute-done | bytes 124960 | tf_op jit(solution)/shard_map/ppermute | solution.py:22
  113.7 4.2 %collective-permute-done.13 = f32[122,1,256]{2,1,0:T(1,128)S(1)} collective-permute-done((f32[122,1,256]{2,1,0:T(1,128)S(1)}, f32[122,1,256]{2,1,0:T(1,128)S(1)}, u32[]{:S(2)}, u32[]{:S(2)}) %collective-permute-start.13) | collective-permute-done | bytes 124960 | tf_op jit(solution)/shard_map/ppermute | solution.py:23
  118.4 1.6 %collective-permute-start.14 = (f32[122,6,1]{2,1,0:T(8,128)S(1)}, f32[122,6,1]{2,1,0:T(8,128)S(1)}, u32[]{:S(2)}, u32[]{:S(2)}) collective-permute-start(f32[122,6,1]{2,1,0:T(8,128)S(1)} %get-tuple-element.88), channel_id=1, source_target_pairs={{0,1},{2,3},{4,5},{6,7},{8,9},{10,11},{12,13},{14,15},{16,17},{18,... | collective-permute-start | bytes 8792 | tf_op jit(solution)/shard_map/ppermute | solution.py:22
  120.0 1.6 %collective-permute-start.15 = (f32[122,6,1]{2,1,0:T(8,128)S(1)}, f32[122,6,1]{2,1,0:T(8,128)S(1)}, u32[]{:S(2)}, u32[]{:S(2)}) collective-permute-start(f32[122,6,1]{2,1,0:T(8,128)S(1)} %get-tuple-element.89), channel_id=1, source_target_pairs={{1,0},{3,2},{5,4},{7,6},{9,8},{11,10},{13,12},{15,14},{17,16},{19,... | collective-permute-start | bytes 8792 | tf_op jit(solution)/shard_map/ppermute | solution.py:23
  121.5 1.6 %exponential_multiply_fusion = f32[36,16,1,256]{3,2,1,0:T(1,128)} fusion(f32[36,16,1,256]{3,2,1,0:T(1,128)S(1)} %get-tuple-element.59, f32[256]{0:T(256)S(1)} %broadcast_multiply_fusion.1, f32[36,16]{1,0:T(8,128)S(1)} %copy.126), kind=kLoop, calls=%fused_computation.80 | loop fusion | flops 294912 | bytes 1182976 | tf_op jit(solution)/shard_map/mul | solution.py:96
  123.7 1.5 %fusion.11 = f32[122,6,258]{2,1,0:T(8,128)S(1)} fusion(f32[1,4,256]{2,1,0:T(4,128)S(1)} %get-tuple-element.129, f32[1,4,256]{2,1,0:T(4,128)S(1)} %get-tuple-element.130, f32[122,6,1]{2,1,0:T(8,128)S(1)} %collective-permute-done.15, f32[122,1,256]{2,1,0:T(1,128)S(1)} %collective-permute-done.13, f32[120,4,256]{2,1,0:T(4,128)S(1)} %copy.119, ...), kind=kLoop, calls=%fused_computation.23 | loop fusion | flops 1133136 | bytes 1510848 | tf_op jit(solution)/shard_map/concatenate | solution.py:24
  125.4 1.1 fusion.109
  126.6 1.4 %fusion.57 = f32[15,8,4,256]{3,0,2,1:T(8,128)S(1)} fusion(f32[15,8,4,256]{3,2,1,0:T(4,128)S(1)} %get-tuple-element.72, f32[15,8,4,256]{3,2,1,0:T(4,128)S(1)} %get-tuple-element.69, f32[15,8,4,256]{3,2,1,0:T(4,128)S(1)} %get-tuple-element.70, f32[15,8,4,256]{3,2,1,0:T(4,128)S(1)} %get-tuple-element.71, f32[15,8,4,256]{3,2,1,0:T(4,128)S(1)} %get-tuple-element.68, ...), kind=kLoop, calls=%fused_computation.102 | loop fusion | flops 1228800 | bytes 2969600 | tf_op jit(solution)/shard_map/add | solution.py:60
  129.5 1.1 copy.127
  (113 shorter events, 18.2 us)
Async XLA Ops:
  0.6 55.7 %copy-start = (f32[15,15]{1,0:T(8,128)S(1)}, f32[15,15]{1,0:T(8,128)}, u32[]{:S(2)}) copy-start(f32[15,15]{1,0:T(8,128)} %param.25) | copy-start | bytes 2704
  0.6 7.4 %copy-start.1 = (f32[36,16,1,256]{3,2,1,0:T(1,128)S(1)}, f32[36,16,1,256]{3,2,1,0:T(1,128)}, u32[]{:S(2)}) copy-start(f32[36,16,1,256]{3,2,1,0:T(1,128)} %param.28) | copy-start | bytes 1769476
  1.7 12.0 %copy-start.2 = (f32[15,8,4,256]{3,2,1,0:T(4,128)S(1)}, f32[15,8,4,256]{3,2,1,0:T(4,128)}, u32[]{:S(2)}) copy-start(f32[15,8,4,256]{3,2,1,0:T(4,128)} %param.19) | copy-start | bytes 1474564
  3.4 4.6 %all-to-all-start = ((f32[2,2,128]{2,0,1:T(2,128)}), f32[2,2,128]{2,0,1:T(2,128)S(1)}, u32[]{:S(2)}, u32[]{:S(2)}) async-start(f32[2,2,128]{2,0,1:T(2,128)} %pad_maximum_fusion.25), calls=%async_computation | async-start | bytes 4096 | tf_op jit(solution)/shard_map/all_to_all | solution.py:123
  10.3 4.8 %collective-permute-start.16 = (f32[36,16,1,256]{3,2,1,0:T(1,128)S(1)}, f32[36,16,1,256]{3,2,1,0:T(1,128)S(1)}, u32[]{:S(2)}, u32[]{:S(2)}) collective-permute-start(f32[36,16,1,256]{3,2,1,0:T(1,128)S(1)} %get-tuple-element.98), channel_id=1, source_target_pairs={{0,1},{1,2},{2,3},{3,4},{4,5},{5,6},{6,7},{7,8},{8,9},{9,10},{10,1... | collective-permute-start | bytes 1769480 | tf_op jit(solution)/shard_map/ppermute | solution.py:22
  12.4 6.2 %collective-permute-start.17 = (f32[36,16,1,256]{3,2,1,0:T(1,128)S(1)}, f32[36,16,1,256]{3,2,1,0:T(1,128)S(1)}, u32[]{:S(2)}, u32[]{:S(2)}) collective-permute-start(f32[36,16,1,256]{3,2,1,0:T(1,128)S(1)} %get-tuple-element.98), channel_id=1, source_target_pairs={{1,0},{2,1},{3,2},{4,3},{5,4},{6,5},{7,6},{8,7},{9,8},{10,9},{11,1... | collective-permute-start | bytes 1769480 | tf_op jit(solution)/shard_map/ppermute | solution.py:23
  18.9 18.0 %copy-start.5 = (s32[4,256]{1,0:T(4,128)S(1)}, s32[4,256]{1,0:T(4,128)}, u32[]{:S(2)}) copy-start(s32[4,256]{1,0:T(4,128)} %param.22) | copy-start | bytes 12292
  18.9 18.0 %copy-start.8 = (f32[2,4,256]{2,1,0:T(4,128)S(1)}, f32[2,4,256]{2,1,0:T(4,128)}, u32[]{:S(2)}) copy-start(f32[2,4,256]{2,1,0:T(4,128)} %param.20) | copy-start | bytes 24580
  36.9 7.9 %collective-permute-start = (f32[122,1,256]{2,0,1:T(8,128)S(1)}, f32[122,1,256]{2,0,1:T(8,128)S(1)}, u32[]{:S(2)}, u32[]{:S(2)}) collective-permute-start(f32[122,1,256]{2,0,1:T(8,128)S(1)} %get-tuple-element.111), channel_id=1, source_target_pairs={{0,2},{2,4},{4,6},{6,8},{8,10},{10,12},{12,14},{1,3},{3,5},{5,7},{... | collective-permute-start | bytes 374792 | tf_op jit(solution)/shard_map/ppermute | solution.py:22
  41.7 10.1 %copy-start.4 = (f32[8,4,256]{2,1,0:T(4,128)S(1)}, f32[8,4,256]{2,1,0:T(4,128)}, u32[]{:S(2)}) copy-start(f32[8,4,256]{2,1,0:T(4,128)} %param.23) | copy-start | bytes 98308
  41.7 7.2 %collective-permute-start.1 = (f32[122,1,256]{2,0,1:T(8,128)S(1)}, f32[122,1,256]{2,0,1:T(8,128)S(1)}, u32[]{:S(2)}, u32[]{:S(2)}) collective-permute-start(f32[122,1,256]{2,0,1:T(8,128)S(1)} %get-tuple-element.112), channel_id=1, source_target_pairs={{2,0},{4,2},{6,4},{8,6},{10,8},{12,10},{14,12},{3,1},{5,3},{7,5},{... | collective-permute-start | bytes 374792 | tf_op jit(solution)/shard_map/ppermute | solution.py:23
  49.2 2.7 %collective-permute-start.2 = (f32[122,6,1]{2,0,1:T(8,128)S(1)}, f32[122,6,1]{2,0,1:T(8,128)S(1)}, u32[]{:S(2)}, u32[]{:S(2)}) collective-permute-start(f32[122,6,1]{2,0,1:T(8,128)S(1)} %get-tuple-element.94), channel_id=1, source_target_pairs={{0,1},{2,3},{4,5},{6,7},{8,9},{10,11},{12,13},{14,15},{16,17},{18,... | collective-permute-start | bytes 8792 | tf_op jit(solution)/shard_map/ppermute | solution.py:22
  50.5 3.6 %collective-permute-start.3 = (f32[122,6,1]{2,0,1:T(8,128)S(1)}, f32[122,6,1]{2,0,1:T(8,128)S(1)}, u32[]{:S(2)}, u32[]{:S(2)}) collective-permute-start(f32[122,6,1]{2,0,1:T(8,128)S(1)} %get-tuple-element.95), channel_id=1, source_target_pairs={{1,0},{3,2},{5,4},{7,6},{9,8},{11,10},{13,12},{15,14},{17,16},{19,... | collective-permute-start | bytes 8792 | tf_op jit(solution)/shard_map/ppermute | solution.py:23
  55.5 1.3 %copy-start.3 = (f32[15,15]{1,0:T(8,128)S(1)}, f32[15,15]{1,0:T(8,128)}, u32[]{:S(2)}) copy-start(f32[15,15]{1,0:T(8,128)} %param.24) | copy-start | bytes 2704
  56.9 0.7 copy-start.6
  57.6 0.7 copy-start.7
  58.3 6.6 %copy-start.9 = (f32[36,16]{0,1:T(8,128)S(1)}, f32[36,16]{0,1:T(8,128)}, u32[]{:S(2)}) copy-start(f32[36,16]{0,1:T(8,128)} %param.29) | copy-start | bytes 6916
  59.1 7.3 %collective-permute-start.4 = (f32[122,1,256]{2,1,0:T(1,128)S(1)}, f32[122,1,256]{2,1,0:T(1,128)S(1)}, u32[]{:S(2)}, u32[]{:S(2)}) collective-permute-start(f32[122,1,256]{2,1,0:T(1,128)S(1)} %get-tuple-element.109), channel_id=1, source_target_pairs={{0,2},{2,4},{4,6},{6,8},{8,10},{10,12},{12,14},{1,3},{3,5},{5,7},{... | collective-permute-start | bytes 374792 | tf_op jit(solution)/shard_map/ppermute | solution.py:22
  63.5 7.0 %collective-permute-start.5 = (f32[122,1,256]{2,1,0:T(1,128)S(1)}, f32[122,1,256]{2,1,0:T(1,128)S(1)}, u32[]{:S(2)}, u32[]{:S(2)}) collective-permute-start(f32[122,1,256]{2,1,0:T(1,128)S(1)} %get-tuple-element.110), channel_id=1, source_target_pairs={{2,0},{4,2},{6,4},{8,6},{10,8},{12,10},{14,12},{3,1},{5,3},{7,5},{... | collective-permute-start | bytes 374792 | tf_op jit(solution)/shard_map/ppermute | solution.py:23
  71.0 3.8 %collective-permute-start.6 = (f32[122,6,1]{2,1,0:T(8,128)S(1)}, f32[122,6,1]{2,1,0:T(8,128)S(1)}, u32[]{:S(2)}, u32[]{:S(2)}) collective-permute-start(f32[122,6,1]{2,1,0:T(8,128)S(1)} %get-tuple-element.92), channel_id=1, source_target_pairs={{0,1},{2,3},{4,5},{6,7},{8,9},{10,11},{12,13},{14,15},{16,17},{18,... | collective-permute-start | bytes 8792 | tf_op jit(solution)/shard_map/ppermute | solution.py:22
  72.3 3.8 %collective-permute-start.7 = (f32[122,6,1]{2,1,0:T(8,128)S(1)}, f32[122,6,1]{2,1,0:T(8,128)S(1)}, u32[]{:S(2)}, u32[]{:S(2)}) collective-permute-start(f32[122,6,1]{2,1,0:T(8,128)S(1)} %get-tuple-element.93), channel_id=1, source_target_pairs={{1,0},{3,2},{5,4},{7,6},{9,8},{11,10},{13,12},{15,14},{17,16},{19,... | collective-permute-start | bytes 8792 | tf_op jit(solution)/shard_map/ppermute | solution.py:23
  83.0 7.1 %collective-permute-start.8 = (f32[122,1,256]{2,1,0:T(1,128)S(1)}, f32[122,1,256]{2,1,0:T(1,128)S(1)}, u32[]{:S(2)}, u32[]{:S(2)}) collective-permute-start(f32[122,1,256]{2,1,0:T(1,128)S(1)} %get-tuple-element.107), channel_id=1, source_target_pairs={{0,2},{2,4},{4,6},{6,8},{8,10},{10,12},{12,14},{1,3},{3,5},{5,7},{... | collective-permute-start | bytes 374792 | tf_op jit(solution)/shard_map/ppermute | solution.py:22
  87.2 7.0 %collective-permute-start.9 = (f32[122,1,256]{2,1,0:T(1,128)S(1)}, f32[122,1,256]{2,1,0:T(1,128)S(1)}, u32[]{:S(2)}, u32[]{:S(2)}) collective-permute-start(f32[122,1,256]{2,1,0:T(1,128)S(1)} %get-tuple-element.108), channel_id=1, source_target_pairs={{2,0},{4,2},{6,4},{8,6},{10,8},{12,10},{14,12},{3,1},{5,3},{7,5},{... | collective-permute-start | bytes 374792 | tf_op jit(solution)/shard_map/ppermute | solution.py:23
  94.8 4.6 %collective-permute-start.10 = (f32[122,6,1]{2,1,0:T(8,128)S(1)}, f32[122,6,1]{2,1,0:T(8,128)S(1)}, u32[]{:S(2)}, u32[]{:S(2)}) collective-permute-start(f32[122,6,1]{2,1,0:T(8,128)S(1)} %get-tuple-element.90), channel_id=1, source_target_pairs={{0,1},{2,3},{4,5},{6,7},{8,9},{10,11},{12,13},{14,15},{16,17},{18,... | collective-permute-start | bytes 8792 | tf_op jit(solution)/shard_map/ppermute | solution.py:22
  96.1 3.8 %collective-permute-start.11 = (f32[122,6,1]{2,1,0:T(8,128)S(1)}, f32[122,6,1]{2,1,0:T(8,128)S(1)}, u32[]{:S(2)}, u32[]{:S(2)}) collective-permute-start(f32[122,6,1]{2,1,0:T(8,128)S(1)} %get-tuple-element.91), channel_id=1, source_target_pairs={{1,0},{3,2},{5,4},{7,6},{9,8},{11,10},{13,12},{15,14},{17,16},{19,... | collective-permute-start | bytes 8792 | tf_op jit(solution)/shard_map/ppermute | solution.py:23
  106.4 7.3 %collective-permute-start.12 = (f32[122,1,256]{2,1,0:T(1,128)S(1)}, f32[122,1,256]{2,1,0:T(1,128)S(1)}, u32[]{:S(2)}, u32[]{:S(2)}) collective-permute-start(f32[122,1,256]{2,1,0:T(1,128)S(1)} %get-tuple-element.105), channel_id=1, source_target_pairs={{0,2},{2,4},{4,6},{6,8},{8,10},{10,12},{12,14},{1,3},{3,5},{5,7},{... | collective-permute-start | bytes 374792 | tf_op jit(solution)/shard_map/ppermute | solution.py:22
  110.3 7.6 %collective-permute-start.13 = (f32[122,1,256]{2,1,0:T(1,128)S(1)}, f32[122,1,256]{2,1,0:T(1,128)S(1)}, u32[]{:S(2)}, u32[]{:S(2)}) collective-permute-start(f32[122,1,256]{2,1,0:T(1,128)S(1)} %get-tuple-element.106), channel_id=1, source_target_pairs={{2,0},{4,2},{6,4},{8,6},{10,8},{12,10},{14,12},{3,1},{5,3},{7,5},{... | collective-permute-start | bytes 374792 | tf_op jit(solution)/shard_map/ppermute | solution.py:23
  118.4 4.8 %collective-permute-start.14 = (f32[122,6,1]{2,1,0:T(8,128)S(1)}, f32[122,6,1]{2,1,0:T(8,128)S(1)}, u32[]{:S(2)}, u32[]{:S(2)}) collective-permute-start(f32[122,6,1]{2,1,0:T(8,128)S(1)} %get-tuple-element.88), channel_id=1, source_target_pairs={{0,1},{2,3},{4,5},{6,7},{8,9},{10,11},{12,13},{14,15},{16,17},{18,... | collective-permute-start | bytes 8792 | tf_op jit(solution)/shard_map/ppermute | solution.py:22
  120.0 3.8 %collective-permute-start.15 = (f32[122,6,1]{2,1,0:T(8,128)S(1)}, f32[122,6,1]{2,1,0:T(8,128)S(1)}, u32[]{:S(2)}, u32[]{:S(2)}) collective-permute-start(f32[122,6,1]{2,1,0:T(8,128)S(1)} %get-tuple-element.89), channel_id=1, source_target_pairs={{1,0},{3,2},{5,4},{7,6},{9,8},{11,10},{13,12},{15,14},{17,16},{19,... | collective-permute-start | bytes 8792 | tf_op jit(solution)/shard_map/ppermute | solution.py:23
where the time goes:
time: 133 us; the launch traced here: 131 us
  starting transfers between devices  40.3 us (30%)
  waiting for transfers between devices  32.6 us (25%)
  other arithmetic  24.8 us (19%)
  local copies, waits for them, and re-layouts  13.3 us (10%)
  blocking collectives  13.1 us (10%)
  matrix products  4.88 us (4%)
  between operations  1.5 us (1%)
    ppermute x9, starting transfers between devices, padded_2(): before = lax.ppermute(last, axis, up)  24.8 us
    ppermute x9, waiting for transfers between devices, padded_2(): after = lax.ppermute(initial, axis, down)  24.5 us
    all_to_all x1, blocking collectives, body(): lax.all_to_all(orbital, 'cross', split_axis=1, concat_axis=0, tiled=True)  13.1 us
    ppermute x9, starting transfers between devices, padded_2(): after = lax.ppermute(initial, axis, down)  12.3 us
    ppermute x9, waiting for transfers between devices, padded_2(): before = lax.ppermute(last, axis, up)  6.84 us
    concatenate x8, other arithmetic, padded_2(): shard = jnp.concatenate([before, shard, after], axis=dim)  5.98 us
    add x4, other arithmetic, advance(): moved_conc = moved_conc + give_south[1:-1, 2:] * padded[:, :, 1:-1, 2:]  5.21 us
    add x1, other arithmetic, finish_waves(): action_density - flux_x - (give_north + give_south) + inflow_x + inflow_y  4.57 us
  transfers between devices with their start and end apart: 19, of which 14 were waited for; matrix products, arithmetic and copies ran while one was open for 5% of the time, Pallas kernels for 0%

commit v1 on v0

v1 whole, which is shorter than its diff:
```python
import functools
import math

import jax
import jax.numpy as jnp
import numpy as np
from jax import lax
from jax.experimental import pallas as pl
from jax.experimental.pallas import tpu as pltpu
from jax.sharding import PartitionSpec as P

SUBSTEPS = 4
GROUPS = 4
diffusion_rate = 0.05
threshold_stress = 0.25
MESH = pl.DeviceIdType.MESH
HIGHEST = lax.Precision.HIGHEST


def roll(x, shift, axis):
    shift = shift % x.shape[axis]
    return x if shift == 0 else pltpu.roll(x, shift, axis)


def iota(shape, dim):
    return lax.broadcasted_iota(jnp.int32, shape, dim)


def kernel(
    classes,
    levels,
    dirs,
    freqs,
    pairs,
    floc_ref,
    cur_ref,
    depth_ref,
    wet_ref,
    shear_ref,
    agg_ref,
    brk_ref,
    settling_ref,
    erosion_ref,
    act_ref,
    wind_ref,
    trig_ref,
    floc_out,
    act_out,
    conc,
    shear,
    coef,
    excess,
    above,
    moved,
    init_send,
    init_recv,
    row_send,
    row_recv,
    col_send,
    col_recv,
    back_send,
    back_recv,
    small_send,
    small_recv,
    flux_send,
    flux_recv,
    prop,
    fields,
    init_sems,
    edge_sems,
    back_sems,
    small_sems,
    flux_sems,
):
    along = lax.axis_index("along")
    core = lax.axis_index("cross")
    x = along % 2
    z = along // 2
    own_half = (x + core) % 2
    per = levels // GROUPS
    layers = classes * per
    sub = iota((8, 128), 0)
    lane = iota((8, 128), 1)
    low = sub < 4

    def same(scalar, value):
        return jnp.full((8, 128), scalar, jnp.int32) == value

    core1 = same(core, 1)
    x1 = same(x, 1)
    pair_id = {"along": along + 1 - 2 * x}
    core_id = {"cross": 1 - core}
    place = x + core * (3 - 2 * x)
    outer_wave = jnp.where(core == 1, along + 1, along - 1)
    has_outer = (outer_wave >= 0) & (outer_wave < 2 * pairs)
    outer_id = {"along": outer_wave, "cross": 1 - core}
    has_low = z > 0
    has_high = z < pairs - 1
    low_id = {"along": along - 2}
    high_id = {"along": along + 2}

    barrier = pltpu.get_barrier_semaphore()
    pl.semaphore_signal(barrier, inc=1, device_id=pair_id, device_id_type=MESH)
    pl.semaphore_signal(barrier, inc=1, device_id=core_id, device_id_type=MESH)

    @pl.when(has_low)
    def _():
        pl.semaphore_signal(barrier, inc=1, device_id=low_id, device_id_type=MESH)

    @pl.when(has_high)
    def _():
        pl.semaphore_signal(barrier, inc=1, device_id=high_id, device_id_type=MESH)

    @pl.when(has_outer)
    def _():
        pl.semaphore_signal(barrier, inc=1, device_id=outer_id, device_id_type=MESH)

    wet = wet_ref[...].astype(jnp.float32)
    east_tile = cur_ref[0] * wet
    north_tile = cur_ref[1] * wet
    depth = depth_ref[...]

    def pack_pair(first, second, take_high):
        return jnp.where(
            take_high,
            jnp.where(low, pltpu.roll(first, 4, 0), second),
            jnp.where(low, first, pltpu.roll(second, 4, 0)),
        )

    send_high = same(own_half, 0)

    def fill(group):
        for k in range(classes):
            init_send[group, pl.ds(8 * k, 8)] = pack_pair(
                floc_ref[k, levels - 1 - 2 * group], floc_ref[k, levels - 2 - 2 * group], send_high
            )
        init_send[group, pl.ds(8 * classes, 8)] = pack_pair(east_tile, north_tile, send_high)
        init_send[group, pl.ds(8 * classes + 8, 8)] = pack_pair(
            shear_ref[levels - 1 - 2 * group], shear_ref[levels - 2 - 2 * group], send_high
        )

    def init_copy(group):
        return pltpu.make_async_remote_copy(
            src_ref=init_send.at[group],
            dst_ref=init_recv.at[group],
            send_sem=init_sems.at[0, group],
            recv_sem=init_sems.at[1, group],
            device_id=pair_id,
            device_id_type=MESH,
        )

    def back_copy(group):
        return pltpu.make_async_remote_copy(
            src_ref=back_send.at[group],
            dst_ref=back_recv.at[group],
            send_sem=back_sems.at[0, group],
            recv_sem=back_sems.at[1, group],
            device_id=pair_id,
            device_id_type=MESH,
        )

    def small_copy(slot, target):
        return pltpu.make_async_remote_copy(
            src_ref=small_send.at[slot],
            dst_ref=small_recv.at[slot],
            send_sem=small_sems.at[0, slot],
            recv_sem=small_sems.at[1, slot],
            device_id=target,
            device_id_type=MESH,
        )

    def row_copy(slot, side, target):
        return pltpu.make_async_remote_copy(
            src_ref=row_send.at[slot, side],
            dst_ref=row_recv.at[slot, side],
            send_sem=edge_sems.at[0, slot, side],
            recv_sem=edge_sems.at[1, slot, side],
            device_id=target,
            device_id_type=MESH,
        )

    def col_copy(slot, side, target):
        return pltpu.make_async_remote_copy(
            src_ref=col_send.at[slot, side],
            dst_ref=col_recv.at[slot, side],
            send_sem=edge_sems.at[0, slot, 2 + side],
            recv_sem=edge_sems.at[1, slot, 2 + side],
            device_id=target,
            device_id_type=MESH,
        )

    up_is_pair = (place == 0) | (place == 2)
    down_is_pair = (place == 1) | (place == 3)
    pair_along = along + 1 - 2 * x
    up_id = {
        "along": jnp.where(up_is_pair, pair_along, along),
        "cross": jnp.where(up_is_pair, core, 1 - core),
    }
    down_id = {
        "along": jnp.where(down_is_pair, pair_along, along),
        "cross": jnp.where(down_is_pair, core, 1 - core),
    }
    has_up = place < 3
    has_down = place > 0

    edges = (
        (has_high, functools.partial(row_copy, side=0, target=high_id)),
        (has_low, functools.partial(row_copy, side=1, target=low_id)),
        (has_up, functools.partial(col_copy, side=0, target=up_id)),
        (has_down, functools.partial(col_copy, side=1, target=down_id)),
    )
    arrives = (has_low, has_high, has_down, has_up)

    lax.fori_loop(0, GROUPS, lambda g, c: (fill(g), c)[1], 0)

    a_in = iota((128, 128), 0)
    b_in = iota((128, 128), 1)
    gather = [jnp.where(a_in // 2 + 64 * j == b_in, 0.25, 0.0).astype(jnp.float32) for j in range(2)]
    spreadm = [jnp.where(a_in == 64 * j + b_in // 2, 1.0, 0.0).astype(jnp.float32) for j in range(2)]

    def coarse(v):
        v = v + pltpu.roll(v, 7, 0)
        c0 = jnp.dot(v, gather[0], precision=HIGHEST, preferred_element_type=jnp.float32)
        c1 = jnp.dot(v, gather[1], precision=HIGHEST, preferred_element_type=jnp.float32)
        return c0 + pltpu.roll(c1, 4, 0)

    depth_c = coarse(depth)
    wet_c = coarse(wet)
    both = jnp.where(sub % 2 == 0, depth_c, pltpu.roll(wet_c, 1, 0))
    mine_c = jnp.where(core1, pltpu.roll(both, 6, 0), both)
    small_send[0] = jnp.where(core1, both, pltpu.roll(both, 6, 0))

    for side, here in enumerate(arrives):

        @pl.when(jnp.logical_not(here))
        def _(side=side):
            def clear(slot, carry):
                if side < 2:
                    row_recv[slot, side] = jnp.zeros((32, 128), jnp.float32)
                else:
                    col_recv[slot, side - 2] = jnp.zeros((8, 128), jnp.float32)
                return carry

            lax.fori_loop(0, SUBSTEPS * GROUPS, clear, 0)

    half_rows = flux_recv.shape[0] // 2
    block = 2 * freqs

    @pl.when(jnp.logical_not(has_outer))
    def _():
        def clear(d, carry):
            start = pl.multiple_of(core * half_rows + d * block, 8)
            flux_recv[pl.ds(start, block)] = jnp.zeros((block, 128), jnp.float32)
            return carry

        lax.fori_loop(0, dirs // 2, clear, 0)

    above[...] = jnp.zeros_like(above)
    excess[...] = jnp.zeros_like(excess)

    waits = 2 + has_low.astype(jnp.int32) + has_high.astype(jnp.int32) + has_outer.astype(jnp.int32)
    pl.semaphore_wait(barrier, waits)
    small_copy(0, core_id).start()
    for g in range(GROUPS):
        init_copy(g).start()

    def add_dir(d, acc):
        return acc + act_ref[pl.ds(pl.multiple_of(d * block, 8), block)]

    total = lax.fori_loop(0, dirs, add_dir, jnp.zeros((block, 128), jnp.float32), unroll=4)

    small_copy(0, core_id).wait_recv()
    other_c = small_recv[0]
    first = jnp.where(core1, other_c, mine_c)
    second = jnp.where(core1, mine_c, other_c)
    even = iota((block, 128), 0) % 2 == 0

    def rows_of(row):
        return jnp.where(
            even,
            jnp.broadcast_to(first[row : row + 1], (block, 128)),
            jnp.broadcast_to(second[row : row + 1], (block, 128)),
        )

    depth_w = rows_of(0)
    wet_w = rows_of(1)
    freq = (iota((block, 128), 0) // 2).astype(jnp.float32)
    shoal = jnp.tanh(depth_w * ((1.0 + 3.0 * freq / freqs) * 0.25))
    speed = 0.45 * shoal * wet_w
    fields[0] = speed
    fields[1] = 0.2 * (1.0 - shoal)

    def sum_rows(v):
        v8 = v[0:8]
        for i in range(1, block // 8):
            v8 = v8 + v[8 * i : 8 * i + 8]
        v8 = v8 + pltpu.roll(v8, 4, 0)
        return v8 + pltpu.roll(v8, 2, 0)

    scale = 1.0 / (dirs * freqs)
    orbital = wet_w[0:8] * (sum_rows(total * (1.0 - shoal * shoal)) * scale)
    flip = pltpu.roll(orbital, 1, 0)
    small_send[1] = jnp.where(core1, orbital, flip)
    small_copy(1, core_id).start()
    mine_o = jnp.where(core1, flip, orbital)

    def flux(d, carry):
        start = pl.multiple_of(d * block, 8)
        flux_send[pl.ds(start, block)] = (trig_ref[0, d] * fields[0]) * act_ref[pl.ds(start, block)]
        return carry

    lax.fori_loop(0, dirs, flux, 0, unroll=2)

    def flux_copy(side, target):
        part = pl.ds(side * half_rows, half_rows)
        return pltpu.make_async_remote_copy(
            src_ref=flux_send.at[part],
            dst_ref=flux_recv.at[part],
            send_sem=flux_sems.at[0, side],
            recv_sem=flux_sems.at[1, side],
            device_id=target,
            device_id_type=MESH,
        )

    @pl.when(core == 0)
    def _():
        flux_copy(0, core_id).start()

    @pl.when(core == 1)
    def _():
        flux_copy(1, core_id).start()

    @pl.when((core == 1) & has_outer)
    def _():
        flux_copy(0, outer_id).start()

    @pl.when((core == 0) & has_outer)
    def _():
        flux_copy(1, outer_id).start()

    small_copy(1, core_id).wait_recv()
    other_o = small_recv[1]
    coarse0 = jnp.where(core1, other_o, mine_o)[0:1]
    coarse1 = jnp.where(core1, mine_o, other_o)[0:1]
    tall = jnp.where(
        sub % 4 < 2, jnp.broadcast_to(coarse0, (8, 128)), jnp.broadcast_to(coarse1, (8, 128))
    )
    fine = jnp.where(
        low,
        jnp.dot(tall, spreadm[0], precision=HIGHEST, preferred_element_type=jnp.float32),
        jnp.dot(tall, spreadm[1], precision=HIGHEST, preferred_element_type=jnp.float32),
    )
    stress = 0.5 * (east_tile * east_tile + north_tile * north_tile) + fine
    excess_tile = wet * jnp.maximum(stress - threshold_stress, 0.0)
    small_send[2] = pack_pair(excess_tile, excess_tile, send_high)
    small_copy(2, pair_id).start()

    my_rows = sub // 4 == jnp.full((8, 128), x, jnp.int32)

    def place_own(v):
        return jnp.where(core1, pltpu.roll(v, 4, 0), v)

    def unpack_pair(first, second, packed):
        turned = pltpu.roll(packed, 4, 0)
        return (
            jnp.where(my_rows, place_own(first), jnp.where(x1, packed, turned)),
            jnp.where(my_rows, place_own(second), jnp.where(x1, turned, packed)),
        )

    def send_edges(group, slot):
        rows = [conc[group, pl.ds(8 * u, 8)] for u in range(layers + 2)]
        row_send[slot, 0] = conc.at[group][pl.ds(7, 32, stride=8), :]
        row_send[slot, 1] = conc.at[group][pl.ds(0, 32, stride=8), :]
        right = jnp.zeros((8, 128), jnp.float32)
        left = jnp.zeros((8, 128), jnp.float32)
        for u, v in enumerate(rows):
            right = jnp.where(lane == u, roll(v, u + 1, 1), right)
            left = jnp.where(lane == u, roll(v, u, 1), left)
        col_send[slot, 0] = right
        col_send[slot, 1] = left
        for here, copy in edges:

            @pl.when(here)
            def _(copy=copy):
                copy(slot).start()

    def begin(group):
        init_copy(group).wait_recv()
        for k in range(classes):
            t0, t1 = unpack_pair(
                floc_ref[k, levels - 1 - 2 * group],
                floc_ref[k, levels - 2 - 2 * group],
                init_recv[group, pl.ds(8 * k, 8)],
            )
            conc[group, pl.ds(16 * k, 8)] = t0
            conc[group, pl.ds(16 * k + 8, 8)] = t1
        e, n = unpack_pair(east_tile, north_tile, init_recv[group, pl.ds(8 * classes, 8)])
        conc[group, pl.ds(8 * layers, 8)] = e
        conc[group, pl.ds(8 * layers + 8, 8)] = n
        s0, s1 = unpack_pair(
            shear_ref[levels - 1 - 2 * group],
            shear_ref[levels - 2 - 2 * group],
            init_recv[group, pl.ds(8 * classes + 8, 8)],
        )
        shear[group, 0] = 0.25 * s0
        shear[group, 1] = 0.25 * s1
        send_edges(group, group)

    begin(0)

    top = sub == 0
    bottom = sub == 7
    first_lane = lane == 0
    last_lane = lane == 127

    def step(t, carry):
        s = t // GROUPS
        g = t % GROUPS

        @pl.when(t < GROUPS - 1)
        def _():
            begin(g + 1)

        for side, (here, (_, copy)) in enumerate(zip(arrives, edges)):

            @pl.when(here)
            def _(copy=copy):
                copy(t).wait_recv()

        from_low = row_recv.at[t, 0]
        from_high = row_recv.at[t, 1]
        from_left = col_recv[t, 0]
        from_right = col_recv[t, 1]

        def neighbours(u, v):
            west = jnp.where(top, from_low[pl.ds(u, 1)], pltpu.roll(v, 1, 0))
            east = jnp.where(bottom, from_high[pl.ds(u, 1)], pltpu.roll(v, 7, 0))
            south = jnp.where(first_lane, roll(from_left, 128 - u, 1), pltpu.roll(v, 1, 1))
            north = jnp.where(last_lane, roll(from_right, 127 - u, 1), pltpu.roll(v, 127, 1))
            return west, east, south, north

        @pl.when(t == 0)
        def _():
            e = conc[0, pl.ds(8 * layers, 8)]
            n = conc[0, pl.ds(8 * layers + 8, 8)]
            e_w, e_e, _, _ = neighbours(layers, e)
            _, _, n_s, n_n = neighbours(layers + 1, n)
            zero = jnp.zeros((8, 128), jnp.float32)

            def rate(v, edge, here):
                give = jnp.maximum(v, 0.0) + diffusion_rate
                return jnp.where(edge & same(here.astype(jnp.int32), 0), zero, give)

            coef[0] = 1.0 - (jnp.abs(e) + jnp.abs(n) + 4.0 * diffusion_rate)
            coef[1] = rate(e_w, top, has_low)
            coef[2] = rate(-e_e, bottom, has_high)
            coef[3] = rate(n_s, first_lane, has_down)
            coef[4] = rate(-n_n, last_lane, has_up)

        @pl.when(t == GROUPS - 1)
        def _():
            small_copy(2, pair_id).wait_recv()
            ex, _ = unpack_pair(excess_tile, excess_tile, small_recv[2])
            excess[...] = ex

        keep, c_w, c_e, c_s, c_n = [coef[i] for i in range(5)]
        for u in range(layers):
            v = conc[g, pl.ds(8 * u, 8)]
            west, east, south, north = neighbours(u, v)
            moved[pl.ds(8 * u, 8)] = (
                keep * v + (c_w * west + c_e * east) + (c_s * south + c_n * north)
            )
        sh = [shear[g, 0], shear[g, 1]]
        last_group = same(g, GROUPS - 1)
        ex = jnp.where(last_group, excess[...], 0.0)
        mv = [moved[pl.ds(8 * u, 8)] for u in range(layers)]
        for k in range(classes):
            mix = [None, None]
            brk = [None, None]
            for m in range(classes):
                a = agg_ref[k, m]
                b = brk_ref[k, m]
                for p in range(2):
                    v = mv[2 * m + p]
                    mix[p] = a * v if m == 0 else mix[p] + a * v
                    brk[p] = b * v if m == 0 else brk[p] + b * v
            r = [
                mv[2 * k + p] + sh[p] * mv[2 * k + p] * mix[p] + 0.25 * brk[p] for p in range(2)
            ]
            w = settling_ref[k]
            top_above = above[pl.ds(8 * k, 8)]
            conc[g, pl.ds(16 * k, 8)] = r[0] - w * r[0] + w * top_above
            conc[g, pl.ds(16 * k + 8, 8)] = r[1] - w * r[1] + w * r[0] + erosion_ref[k] * ex
            above[pl.ds(8 * k, 8)] = jnp.where(last_group, 0.0, r[1])

        @pl.when(s < SUBSTEPS - 1)
        def _():
            send_edges(g, t + GROUPS)

        @pl.when(s == SUBSTEPS - 1)
        def _():
            for k in range(classes):
                back_send[g, pl.ds(8 * k, 8)] = pack_pair(
                    conc[g, pl.ds(16 * k, 8)], conc[g, pl.ds(16 * k + 8, 8)], same(x, 0)
                )
            back_copy(g).start()

        return carry

    lax.fori_loop(0, SUBSTEPS * GROUPS, step, 0)

    @pl.when((core == 1) | has_outer)
    def _():
        flux_copy(0, core_id).wait_recv()

    @pl.when((core == 0) | has_outer)
    def _():
        flux_copy(1, core_id).wait_recv()

    wide_lane = iota((block, 128), 1)

    def propagate(northward, d, acc):
        start = pl.multiple_of(d * block, 8)
        a = act_ref[pl.ds(start, block)]
        give = (trig_ref[1, d] * fields[0]) * a
        if northward:
            r = pltpu.roll(give, 1, 1)
            fix = jnp.where(even, 0.0, pltpu.roll(r, 1, 0))
            inflow = jnp.where(wide_lane == 0, fix, r)
        else:
            r = pltpu.roll(give, 127, 1)
            fix = jnp.where(even, pltpu.roll(r, block - 1, 0), 0.0)
            inflow = jnp.where(wide_lane == 127, fix, r)
        p = a - flux_send[pl.ds(start, block)] - give + flux_recv[pl.ds(start, block)] + inflow
        prop[pl.ds(start, block)] = p
        return acc + p

    quarter = dirs // 4
    acc = jnp.zeros((block, 128), jnp.float32)
    acc = lax.fori_loop(0, quarter, functools.partial(propagate, False), acc)
    acc = lax.fori_loop(quarter, 3 * quarter, functools.partial(propagate, True), acc)
    acc = lax.fori_loop(3 * quarter, dirs, functools.partial(propagate, False), acc)
    decay = jnp.exp(-0.5 * (sum_rows(acc) * scale))
    decay = jnp.concatenate([decay] * (block // 8), axis=0)
    grow = jnp.exp(wind_ref[...])
    pick = jnp.where(iota((block, freqs), 0) // 2 == iota((block, freqs), 1), 1.0, 0.0)
    grow = jnp.dot(
        pick.astype(jnp.float32), grow, precision=HIGHEST, preferred_element_type=jnp.float32
    )
    turning = fields[1]

    def finish(d, g):
        before = jnp.where(d == 0, dirs - 1, d - 1)
        after = jnp.where(d == dirs - 1, 0, d + 1)
        p = prop[pl.ds(pl.multiple_of(d * block, 8), block)]
        pb = prop[pl.ds(pl.multiple_of(before * block, 8), block)]
        pa = prop[pl.ds(pl.multiple_of(after * block, 8), block)]
        spread = p + turning * (pb + pa - 2.0 * p)
        factor = jnp.broadcast_to(g[:, 0:1], (block, 128)) * decay
        act_out[pl.ds(pl.multiple_of(d * block, 8), block)] = spread * factor
        return pltpu.roll(g, 127, 1)

    lax.fori_loop(0, dirs, finish, grow)

    own = sub // 4 == jnp.full((8, 128), own_half, jnp.int32)
    own1 = same(own_half, 1)

    def gather_back(g, carry):
        back_copy(g).wait_recv()
        for k in range(classes):
            packed = back_recv[g, pl.ds(8 * k, 8)]
            turned = pltpu.roll(packed, 4, 0)
            t0 = place_own(conc[g, pl.ds(16 * k, 8)])
            t1 = place_own(conc[g, pl.ds(16 * k + 8, 8)])
            floc_out[k, levels - 1 - 2 * g] = jnp.where(
                own, t0, jnp.where(own1, packed, turned)
            )
            floc_out[k, levels - 2 - 2 * g] = jnp.where(
                own, t1, jnp.where(own1, turned, packed)
            )
        return carry

    lax.fori_loop(0, GROUPS, gather_back, 0)

    small_copy(0, core_id).wait_send()
    small_copy(1, core_id).wait_send()
    small_copy(2, pair_id).wait_send()

    def drain_groups(g, carry):
        init_copy(g).wait_send()
        back_copy(g).wait_send()
        return carry

    lax.fori_loop(0, GROUPS, drain_groups, 0)

    def drain_edges(t, carry):
        for here, copy in edges:

            @pl.when(here)
            def _(copy=copy):
                copy(t).wait_send()

        return carry

    lax.fori_loop(0, SUBSTEPS * GROUPS, drain_edges, 0)

    @pl.when((core == 0) | has_outer)
    def _():
        flux_copy(0, core_id).wait_send()

    @pl.when((core == 1) | has_outer)
    def _():
        flux_copy(1, core_id).wait_send()


def halves(tile):
    rows = tile.shape[-2]
    split = tile.reshape(tile.shape[:-1] + (2, 128))
    return jnp.swapaxes(split, -3, -2).reshape(tile.shape[:-2] + (2 * rows, 128))


def unhalves(tile):
    rows = tile.shape[-2] // 2
    split = tile.reshape(tile.shape[:-2] + (2, rows, 128))
    return jnp.swapaxes(split, -3, -2).reshape(tile.shape[:-2] + (rows, 256))


def body(
    pairs,
    floc_conc,
    currents,
    water_depth,
    wet_mask,
    shear_rate,
    aggregation,
    breakup,
    settling,
    erosion,
    action_density,
    wind_growth,
):
    classes, levels = floc_conc.shape[:2]
    dirs, freqs = wind_growth.shape
    rows = dirs * freqs * 2
    angles = (np.arange(dirs) + 0.5) * (2.0 * math.pi / dirs) - 0.5 * math.pi
    trig = jnp.asarray(np.abs(np.stack([np.cos(angles), np.sin(angles)])).astype(np.float32))
    wind = jnp.pad(wind_growth.T, ((0, 0), (0, 128 - dirs)))
    vmem = pl.BlockSpec(memory_space=pltpu.VMEM)
    smem = pl.BlockSpec(memory_space=pltpu.SMEM)
    slots = SUBSTEPS * GROUPS
    f32 = jnp.float32
    V = pltpu.VMEM
    out_floc, out_act = pl.pallas_call(
        functools.partial(kernel, classes, levels, dirs, freqs, pairs),
        out_shape=(
            jax.ShapeDtypeStruct((classes, levels, 8, 128), f32),
            jax.ShapeDtypeStruct((rows, 128), f32),
        ),
        in_specs=[vmem] * 5 + [smem] * 4 + [vmem, vmem, smem],
        out_specs=(vmem, vmem),
        scratch_shapes=[
            V((GROUPS, 32 * 8, 128), f32),
            V((GROUPS, 2, 8, 128), f32),
            V((5, 8, 128), f32),
            V((8, 128), f32),
            V((classes * 8, 128), f32),
            V((classes * 16, 128), f32),
            V((GROUPS, classes * 8 + 16, 128), f32),
            V((GROUPS, classes * 8 + 16, 128), f32),
            V((slots, 2, 32, 128), f32),
            V((slots, 2, 32, 128), f32),
            V((slots, 2, 8, 128), f32),
            V((slots, 2, 8, 128), f32),
            V((GROUPS, classes * 8, 128), f32),
            V((GROUPS, classes * 8, 128), f32),
            V((3, 8, 128), f32),
            V((3, 8, 128), f32),
            V((rows, 128), f32),
            V((rows, 128), f32),
            V((rows, 128), f32),
            V((2, 2 * freqs, 128), f32),
            pltpu.SemaphoreType.DMA((2, GROUPS)),
            pltpu.SemaphoreType.DMA((2, slots, 4)),
            pltpu.SemaphoreType.DMA((2, GROUPS)),
            pltpu.SemaphoreType.DMA((2, 3)),
            pltpu.SemaphoreType.DMA((2, 2)),
        ],
        compiler_params=pltpu.CompilerParams(
            collective_id=0, has_side_effects=True, vmem_limit_bytes=32 * 1024 * 1024
        ),
    )(
        halves(floc_conc),
        halves(currents),
        halves(water_depth),
        halves(wet_mask),
        halves(shear_rate),
        aggregation,
        breakup,
        settling,
        erosion,
        action_density.reshape(rows, 128),
        wind,
        trig,
    )
    return unhalves(out_floc), out_act.reshape(action_density.shape)


def solution(mesh):
    placed = (
        P(None, None, ("group", "along"), "cross"),
        P(None, ("group", "along"), "cross"),
        P(("group", "along"), "cross"),
        P(("group", "along"), "cross"),
        P(None, ("group", "along"), "cross"),
        P(),
        P(),
        P(),
        P(),
        P(None, None, ("group", "along", "cross"), None),
        P(),
    )
    return jax.shard_map(
        functools.partial(body, mesh.shape["along"] // 2),
        mesh=mesh,
        in_specs=placed,
        out_specs=(
            P(None, None, ("group", "along"), "cross"),
            P(None, None, ("group", "along", "cross"), None),
        ),
        check_vma=False,
    )
```

time: 133 us -> 50.5 us (0.38); the launches traced: 131 us -> 50.1 us
  Pallas kernels: 0 us -> 42.9 us
  starting transfers between devices: 40.3 us -> 0 us
  waiting for transfers between devices: 32.6 us -> 0 us
  other arithmetic: 24.8 us -> 0 us
  blocking collectives: 13.1 us -> 0 us
  local copies, waits for them, and re-layouts: 13.3 us -> 6.54 us
  matrix products: 4.88 us -> 0 us
    pallas_call x0 -> x1, Pallas kernels: none -> 42.9 us  [body(): pl.pallas_call(functools.partial(kernel, classes, levels, dirs, freqs, pa...]
    ppermute x18 -> x0, starting transfers between devices: 37.1 us -> none  [the longest x9 24.8 us: padded_2(): before = lax.ppermute(last, axis, up)]
    ppermute x18 -> x0, waiting for transfers between devices: 31.4 us -> none  [the longest x9 24.5 us: padded_2(): after = lax.ppermute(initial, axis, down)]
    all_to_all x1 -> x0, blocking collectives: 13.1 us -> none  [body(): lax.all_to_all(orbital, 'cross', split_axis=1, concat_axis=0, tiled=True)]
    add x13 -> x0, other arithmetic: 10.8 us -> none  [the longest x4 5.21 us: advance(): moved_conc = moved_conc + give_south[1:-1, 2:] * padded[:, :, 1:-1, 2:]]
    slice x24 -> x0, local copies, waits for them, and re-layouts: 8.58 us -> none  [the longest x4 4 us: advance(): centre = padded[:, :, 1:-1, 1:-1]]
    concatenate x11 -> x0, other arithmetic: 6.31 us -> none  [the longest x8 5.98 us: padded_2(): shard = jnp.concatenate([before, shard, after], axis=dim)]
    dot_general x8 -> x0, matrix products: 4.88 us -> none  [the longest x4 2.6 us: advance(): jnp.einsum('kc,clxy->klxy', aggregation, moved_conc, precision=lax.Precis...]
  transfers between devices with their start and end apart: 19 -> 0, of which waited for: 14 -> 0; matrix products, arithmetic and copies ran while one was open for 5% -> 0% of each run, Pallas kernels for 0% -> 0%
where the time goes in v1:
time: 50.5 us; the launch traced here: 50.1 us
  Pallas kernels  42.9 us (85%)
  local copies, waits for them, and re-layouts  6.54 us (13%)
  between operations  0.73 us (1%)
    pallas_call x1, Pallas kernels, body(): pl.pallas_call(functools.partial(kernel, classes, levels, dirs, freqs, pa...  42.9 us
    unnamed x24, local copies, waits for them, and re-layouts  5.81 us

profile of v1, /device:TPU:0, one launch (start us, length us, event | category | flops | bytes accessed | tf_op | source)
XLA Modules:
  0.0 50.1 jit_solution(2811305737722190865)
XLA Ops:
  0.6 0.0 copy-start.6
  0.6 0.0 copy-start.8
  0.7 0.0 copy-start.9
  0.7 0.0 copy-start.5
  0.7 0.0 copy-start.3
  0.7 0.0 copy-start.4
  0.7 0.7 %pad.4.wind_ref = f32[16,128]{1,0:T(8,128)S(1)} pad(f32[16,36]{1,0:T(8,128)} %bitcast.41, f32[]{:T(128)} %constant.4.clone.1), padding=0_0x0_92 | pad | bytes 10500 | tf_op jit(solution)/shard_map/jit(_pad)/pad | solution.py:647
  1.4 0.0 copy-done.6
  1.4 0.0 copy-done.8
  1.4 0.0 copy-done.9
  1.4 0.0 copy-done.5
  1.4 0.0 copy-done.3
  1.5 0.0 copy-done.4
  1.5 0.0 copy-start
  1.5 1.1 %copy-done = f32[36,16,1,256]{3,2,1,0:T(1,128)S(1)} copy-done((f32[36,16,1,256]{3,2,1,0:T(1,128)S(1)}, f32[36,16,1,256]{3,2,1,0:T(1,128)}, u32[]{:S(2)}) %copy-start) | copy-done | bytes 589848
  2.5 0.0 copy-start.1
  2.5 1.0 %copy-done.1 = f32[15,8,4,256]{3,2,1,0:T(4,128)S(1)} copy-done((f32[15,8,4,256]{3,2,1,0:T(4,128)S(1)}, f32[15,8,4,256]{3,2,1,0:T(4,128)}, u32[]{:S(2)}) %copy-start.1) | copy-done | bytes 491544
  3.6 0.0 copy-start.2
  3.6 0.8 %copy-done.2 = f32[8,4,256]{2,1,0:T(4,128)S(1)} copy-done((f32[8,4,256]{2,1,0:T(4,128)S(1)}, f32[8,4,256]{2,1,0:T(4,128)}, u32[]{:S(2)}) %copy-start.2) | copy-done | bytes 32792
  4.3 0.0 copy-start.7
  4.3 0.7 %copy-done.7 = s32[4,256]{1,0:T(4,128)S(1)} copy-done((s32[4,256]{1,0:T(4,128)S(1)}, s32[4,256]{1,0:T(4,128)}, u32[]{:S(2)}) %copy-start.7) | copy-done | bytes 4120
  5.0 0.0 copy-start.10
  5.0 0.7 %copy-done.10 = f32[15]{0:T(128)S(1)} copy-done((f32[15]{0:T(128)S(1)}, f32[15]{0:T(128)}, u32[]{:S(2)}) %copy-start.10) | copy-done | bytes 84
  5.7 42.9 %shard_map.131 = (f32[15,8,8,128]{3,2,1,0:T(8,128)S(1)}, f32[1152,128]{1,0:T(8,128)S(1)}) custom-call(f32[15,8,8,128]{3,2,1,0:T(8,128)S(1)} %bitcast.35, f32[2,8,128]{2,1,0:T(8,128)S(1)} %bitcast.38, f32[8,128]{1,0:T(8,128)S(1)} %bitcast.39, s32[8,128]{1,0:T(8,128)S(1)} %bitcast.40, f32[8,8,128]{2,1,0:T(8,128)S(1)} %bitcast.37, f32[15,15]{1,0:T(8,128)S(1)} %copy-done.4, ...), custom_call_target="tpu_custom_call" | custom-call | tf_op jit(solution)/shard_map/pallas_call | solution.py:653
  48.5 0.8 %copy.23 = f32[15,8,4,256]{3,2,1,0:T(4,128)} copy(f32[15,8,4,256]{3,2,1,0:T(4,128)S(1)} %bitcast.36) | data formatting | bytes 983040
  49.3 0.8 %copy.24 = f32[36,16,1,256]{3,2,1,0:T(1,128)} copy(f32[36,16,1,256]{3,2,1,0:T(1,128)S(1)} %bitcast.34) | data formatting | bytes 1179648
Async XLA Ops:
  0.6 0.8 %copy-start.6 = (f32[4,256]{1,0:T(4,128)S(1)}, f32[4,256]{1,0:T(4,128)}, u32[]{:S(2)}) copy-start(f32[4,256]{1,0:T(4,128)} %param.14) | copy-start | bytes 12292
  0.6 0.8 %copy-start.8 = (f32[2,36]{1,0:T(2,128)S(1)}, f32[2,36]{1,0:T(2,128)}, u32[]{:S(2)}) copy-start(f32[2,36]{1,0:T(2,128)} %constant.5.clone.trig_ref) | copy-start | bytes 868
  0.7 0.8 %copy-start.9 = (f32[15]{0:T(128)S(1)}, f32[15]{0:T(128)}, u32[]{:S(2)}) copy-start(f32[15]{0:T(128)} %settling_ref.1) | copy-start | bytes 184
  0.7 0.8 %copy-start.5 = (f32[15,15]{1,0:T(8,128)S(1)}, f32[15,15]{1,0:T(8,128)}, u32[]{:S(2)}) copy-start(f32[15,15]{1,0:T(8,128)} %brk_ref.1) | copy-start | bytes 2704
  0.7 0.8 %copy-start.3 = (f32[2,4,256]{2,1,0:T(4,128)S(1)}, f32[2,4,256]{2,1,0:T(4,128)}, u32[]{:S(2)}) copy-start(f32[2,4,256]{2,1,0:T(4,128)} %param.13) | copy-start | bytes 24580
  0.7 0.8 %copy-start.4 = (f32[15,15]{1,0:T(8,128)S(1)}, f32[15,15]{1,0:T(8,128)}, u32[]{:S(2)}) copy-start(f32[15,15]{1,0:T(8,128)} %agg_ref.1) | copy-start | bytes 2704
  1.5 1.1 %copy-start = (f32[36,16,1,256]{3,2,1,0:T(1,128)S(1)}, f32[36,16,1,256]{3,2,1,0:T(1,128)}, u32[]{:S(2)}) copy-start(f32[36,16,1,256]{3,2,1,0:T(1,128)} %param.21) | copy-start | bytes 1769476
  2.5 1.0 %copy-start.1 = (f32[15,8,4,256]{3,2,1,0:T(4,128)S(1)}, f32[15,8,4,256]{3,2,1,0:T(4,128)}, u32[]{:S(2)}) copy-start(f32[15,8,4,256]{3,2,1,0:T(4,128)} %param.12) | copy-start | bytes 1474564
  3.6 0.8 %copy-start.2 = (f32[8,4,256]{2,1,0:T(4,128)S(1)}, f32[8,4,256]{2,1,0:T(4,128)}, u32[]{:S(2)}) copy-start(f32[8,4,256]{2,1,0:T(4,128)} %param.16) | copy-start | bytes 98308
  4.3 0.7 %copy-start.7 = (s32[4,256]{1,0:T(4,128)S(1)}, s32[4,256]{1,0:T(4,128)}, u32[]{:S(2)}) copy-start(s32[4,256]{1,0:T(4,128)} %param.15) | copy-start | bytes 12292
  5.0 0.7 %copy-start.10 = (f32[15]{0:T(128)S(1)}, f32[15]{0:T(128)}, u32[]{:S(2)}) copy-start(f32[15]{0:T(128)} %erosion_ref.1) | copy-start | bytes 184

commit v2 on v1

--- a/solution.py
+++ b/solution.py
@@ -11,6 +11,7 @@
 
 SUBSTEPS = 4
 GROUPS = 4
+CHUNKS = 8
 diffusion_rate = 0.05
 threshold_stress = 0.25
 MESH = pl.DeviceIdType.MESH
@@ -32,18 +33,18 @@
     dirs,
     freqs,
     pairs,
-    floc_ref,
-    cur_ref,
-    depth_ref,
-    wet_ref,
-    shear_ref,
-    agg_ref,
-    brk_ref,
-    settling_ref,
-    erosion_ref,
-    act_ref,
-    wind_ref,
-    trig_ref,
+    floc_hbm,
+    cur_hbm,
+    depth_hbm,
+    wet_hbm,
+    shear_hbm,
+    agg_hbm,
+    brk_hbm,
+    settling_hbm,
+    erosion_hbm,
+    act_hbm,
+    wind_hbm,
+    trig_hbm,
     floc_out,
     act_out,
     conc,
@@ -66,6 +67,22 @@
     flux_recv,
     prop,
     fields,
+    growth,
+    wave_sum,
+    decay_ref,
+    floc_ref,
+    cur_ref,
+    depth_ref,
+    wet_ref,
+    shear_ref,
+    agg_ref,
+    brk_ref,
+    settling_ref,
+    erosion_ref,
+    act_ref,
+    wind_ref,
+    trig_ref,
+    load_sems,
     init_sems,
     edge_sems,
     back_sems,
@@ -99,6 +116,25 @@
     low_id = {"along": along - 2}
     high_id = {"along": along + 2}
 
+    loads = [
+        pltpu.make_async_copy(src, dst, load_sems.at[i])
+        for i, (src, dst) in enumerate(
+            (
+                (wet_hbm, wet_ref),
+                (cur_hbm, cur_ref),
+                (depth_hbm, depth_ref),
+                (shear_hbm, shear_ref),
+                (floc_hbm, floc_ref),
+                (act_hbm, act_ref),
+                (trig_hbm, trig_ref),
+                (agg_hbm, agg_ref),
+                (brk_hbm, brk_ref),
+                (settling_hbm, settling_ref),
+                (erosion_hbm, erosion_ref),
+                (wind_hbm, wind_ref),
+            )
+        )
+    ]
     barrier = pltpu.get_barrier_semaphore()
     pl.semaphore_signal(barrier, inc=1, device_id=pair_id, device_id_type=MESH)
     pl.semaphore_signal(barrier, inc=1, device_id=core_id, device_id_type=MESH)
@@ -114,6 +150,11 @@
     @pl.when(has_outer)
     def _():
         pl.semaphore_signal(barrier, inc=1, device_id=outer_id, device_id_type=MESH)
+
+    for load in loads:
+        load.start()
+    for load in loads[:4]:
+        load.wait()
 
     wet = wet_ref[...].astype(jnp.float32)
     east_tile = cur_ref[0] * wet
@@ -211,8 +252,6 @@
     )
     arrives = (has_low, has_high, has_down, has_up)
 
-    lax.fori_loop(0, GROUPS, lambda g, c: (fill(g), c)[1], 0)
-
     a_in = iota((128, 128), 0)
     b_in = iota((128, 128), 1)
     gather = [jnp.where(a_in // 2 + 64 * j == b_in, 0.25, 0.0).astype(jnp.float32) for j in range(2)]
@@ -245,6 +284,26 @@
 
     half_rows = flux_recv.shape[0] // 2
     block = 2 * freqs
+    chunk_rows = half_rows // CHUNKS
+    flux_goes = ((core == 0) | has_outer, (core == 1) | has_outer)
+    flux_comes = ((core == 1) | has_outer, (core == 0) | has_outer)
+    flux_along = (
+        jnp.where(core == 0, along, along + 1),
+        jnp.where(core == 1, along, along - 1),
+    )
+
+    def flux_copy(side, chunk):
+        start = side * half_rows + chunk * chunk_rows
+        part = pl.ds(pl.multiple_of(start, 8), chunk_rows)
+        return pltpu.make_async_remote_copy(
+            src_ref=flux_send.at[part],
+            dst_ref=flux_recv.at[part],
+            send_sem=flux_sems.at[0, side, chunk],
+            recv_sem=flux_sems.at[1, side, chunk],
+            device_id={"along": flux_along[side], "cross": 1 - core},
+            device_id_type=MESH,
+        )
+
 
     @pl.when(jnp.logical_not(has_outer))
     def _():
@@ -258,11 +317,21 @@
     above[...] = jnp.zeros_like(above)
     excess[...] = jnp.zeros_like(excess)
 
+    loads[4].wait()
+    fill(0)
     waits = 2 + has_low.astype(jnp.int32) + has_high.astype(jnp.int32) + has_outer.astype(jnp.int32)
     pl.semaphore_wait(barrier, waits)
     small_copy(0, core_id).start()
-    for g in range(GROUPS):
+    init_copy(0).start()
+
+    def fill_and_send(g, carry):
+        fill(g)
         init_copy(g).start()
+        return carry
+
+    lax.fori_loop(1, GROUPS, fill_and_send, 0)
+    loads[5].wait()
+    loads[6].wait()
 
     def add_dir(d, acc):
         return acc + act_ref[pl.ds(pl.multiple_of(d * block, 8), block)]
@@ -303,57 +372,6 @@
     small_send[1] = jnp.where(core1, orbital, flip)
     small_copy(1, core_id).start()
     mine_o = jnp.where(core1, flip, orbital)
-
-    def flux(d, carry):
-        start = pl.multiple_of(d * block, 8)
-        flux_send[pl.ds(start, block)] = (trig_ref[0, d] * fields[0]) * act_ref[pl.ds(start, block)]
-        return carry
-
-    lax.fori_loop(0, dirs, flux, 0, unroll=2)
-
-    def flux_copy(side, target):
-        part = pl.ds(side * half_rows, half_rows)
-        return pltpu.make_async_remote_copy(
-            src_ref=flux_send.at[part],
-            dst_ref=flux_recv.at[part],
-            send_sem=flux_sems.at[0, side],
-            recv_sem=flux_sems.at[1, side],
-            device_id=target,
-            device_id_type=MESH,
-        )
-
-    @pl.when(core == 0)
-    def _():
-        flux_copy(0, core_id).start()
-
-    @pl.when(core == 1)
-    def _():
-        flux_copy(1, core_id).start()
-
-    @pl.when((core == 1) & has_outer)
-    def _():
-        flux_copy(0, outer_id).start()
-
-    @pl.when((core == 0) & has_outer)
-    def _():
-        flux_copy(1, outer_id).start()
-
-    small_copy(1, core_id).wait_recv()
-    other_o = small_recv[1]
-    coarse0 = jnp.where(core1, other_o, mine_o)[0:1]
-    coarse1 = jnp.where(core1, mine_o, other_o)[0:1]
-    tall = jnp.where(
-        sub % 4 < 2, jnp.broadcast_to(coarse0, (8, 128)), jnp.broadcast_to(coarse1, (8, 128))
-    )
-    fine = jnp.where(
-        low,
-        jnp.dot(tall, spreadm[0], precision=HIGHEST, preferred_element_type=jnp.float32),
-        jnp.dot(tall, spreadm[1], precision=HIGHEST, preferred_element_type=jnp.float32),
-    )
-    stress = 0.5 * (east_tile * east_tile + north_tile * north_tile) + fine
-    excess_tile = wet * jnp.maximum(stress - threshold_stress, 0.0)
-    small_send[2] = pack_pair(excess_tile, excess_tile, send_high)
-    small_copy(2, pair_id).start()
 
     my_rows = sub // 4 == jnp.full((8, 128), x, jnp.int32)
 
@@ -408,6 +426,117 @@
 
     begin(0)
 
+    def flux(d, carry):
+        start = pl.multiple_of(d * block, 8)
+        flux_send[pl.ds(start, block)] = (trig_ref[0, d] * fields[0]) * act_ref[pl.ds(start, block)]
+        return carry
+
+    lax.fori_loop(0, dirs, flux, 0, unroll=4)
+
+    for load in loads[7:]:
+        load.wait()
+
+    widen = jnp.where(iota((dirs, 128), 0) == iota((dirs, 128), 1), 1.0, 0.0)
+    grow = jnp.dot(
+        jnp.exp(wind_ref[...]),
+        widen.astype(jnp.float32),
+        precision=HIGHEST,
+        preferred_element_type=jnp.float32,
+    )
+    pick = jnp.where(iota((block, freqs), 0) // 2 == iota((block, freqs), 1), 1.0, 0.0)
+    grow = jnp.dot(
+        pick.astype(jnp.float32), grow, precision=HIGHEST, preferred_element_type=jnp.float32
+    )
+    growth[...] = grow
+    wave_sum[...] = jnp.zeros_like(wave_sum)
+
+
+    small_copy(1, core_id).wait_recv()
+    other_o = small_recv[1]
+    coarse0 = jnp.where(core1, other_o, mine_o)[0:1]
+    coarse1 = jnp.where(core1, mine_o, other_o)[0:1]
+    tall = jnp.where(
+        sub % 4 < 2, jnp.broadcast_to(coarse0, (8, 128)), jnp.broadcast_to(coarse1, (8, 128))
+    )
+    fine = jnp.where(
+        low,
+        jnp.dot(tall, spreadm[0], precision=HIGHEST, preferred_element_type=jnp.float32),
+        jnp.dot(tall, spreadm[1], precision=HIGHEST, preferred_element_type=jnp.float32),
+    )
+    stress = 0.5 * (east_tile * east_tile + north_tile * north_tile) + fine
+    excess_tile = wet * jnp.maximum(stress - threshold_stress, 0.0)
+    small_send[2] = pack_pair(excess_tile, excess_tile, send_high)
+    small_copy(2, pair_id).start()
+
+    quarter = dirs // 4
+    wide_lane = iota((block, 128), 1)
+
+    def propagate(northward, q):
+        def one(i, acc):
+            d = q * quarter + i
+            start = pl.multiple_of(d * block, 8)
+            a = act_ref[pl.ds(start, block)]
+            give = (trig_ref[1, d] * fields[0]) * a
+            if northward:
+                r = pltpu.roll(give, 1, 1)
+                fix = jnp.where(even, 0.0, pltpu.roll(r, 1, 0))
+                inflow = jnp.where(wide_lane == 0, fix, r)
+            else:
+                r = pltpu.roll(give, 127, 1)
+                fix = jnp.where(even, pltpu.roll(r, block - 1, 0), 0.0)
+                inflow = jnp.where(wide_lane == 127, fix, r)
+            p = a - flux_send[pl.ds(start, block)] - give + flux_recv[pl.ds(start, block)] + inflow
+            prop[pl.ds(start, block)] = p
+            return acc + p
+
+        wave_sum[...] = lax.fori_loop(0, quarter, one, wave_sum[...], unroll=3)
+
+    def finish(q):
+        turning = fields[1]
+
+        def one(i, g):
+            d = q * quarter + i
+            before = jnp.where(d == 0, dirs - 1, d - 1)
+            after = jnp.where(d == dirs - 1, 0, d + 1)
+            p = prop[pl.ds(pl.multiple_of(d * block, 8), block)]
+            pb = prop[pl.ds(pl.multiple_of(before * block, 8), block)]
+            pa = prop[pl.ds(pl.multiple_of(after * block, 8), block)]
+            spread = p + turning * (pb + pa - 2.0 * p)
+            factor = jnp.broadcast_to(g[:, 0:1], (block, 128)) * decay_ref[...]
+            act_out[pl.ds(pl.multiple_of(d * block, 8), block)] = spread * factor
+            return pltpu.roll(g, 127, 1)
+
+        growth[...] = lax.fori_loop(0, quarter, one, growth[...], unroll=3)
+
+    def waves(t):
+        @pl.when(t < CHUNKS)
+        def _():
+            for side in range(2):
+
+                @pl.when(flux_goes[side])
+                def _(side=side):
+                    flux_copy(side, t).start()
+
+        for part in range(4):
+
+            @pl.when(t == CHUNKS + part)
+            def _(part=part):
+                @pl.when(flux_comes[part // 2])
+                def _():
+                    for i in range(CHUNKS // 2):
+                        flux_copy(part // 2, part % 2 * (CHUNKS // 2) + i).wait_recv()
+
+                propagate(part in (1, 2), part)
+
+        @pl.when(t == CHUNKS + 4)
+        def _():
+            decay = jnp.exp(-0.5 * (sum_rows(wave_sum[...]) * scale))
+            decay_ref[...] = jnp.concatenate([decay] * (block // 8), axis=0)
+
+        @pl.when(t >= CHUNKS + 4)
+        def _():
+            finish(t - CHUNKS - 4)
+
     top = sub == 0
     bottom = sub == 7
     first_lane = lane == 0
@@ -420,6 +549,8 @@
         @pl.when(t < GROUPS - 1)
         def _():
             begin(g + 1)
+
+        waves(t)
 
         for side, (here, (_, copy)) in enumerate(zip(arrives, edges)):
 
@@ -509,59 +640,6 @@
 
     lax.fori_loop(0, SUBSTEPS * GROUPS, step, 0)
 
-    @pl.when((core == 1) | has_outer)
-    def _():
-        flux_copy(0, core_id).wait_recv()
-
-    @pl.when((core == 0) | has_outer)
-    def _():
-        flux_copy(1, core_id).wait_recv()
-
-    wide_lane = iota((block, 128), 1)
-
-    def propagate(northward, d, acc):
-        start = pl.multiple_of(d * block, 8)
-        a = act_ref[pl.ds(start, block)]
-        give = (trig_ref[1, d] * fields[0]) * a
-        if northward:
-            r = pltpu.roll(give, 1, 1)
-            fix = jnp.where(even, 0.0, pltpu.roll(r, 1, 0))
-            inflow = jnp.where(wide_lane == 0, fix, r)
-        else:
-            r = pltpu.roll(give, 127, 1)
-            fix = jnp.where(even, pltpu.roll(r, block - 1, 0), 0.0)
-            inflow = jnp.where(wide_lane == 127, fix, r)
-        p = a - flux_send[pl.ds(start, block)] - give + flux_recv[pl.ds(start, block)] + inflow
-        prop[pl.ds(start, block)] = p
-        return acc + p
-
-    quarter = dirs // 4
-    acc = jnp.zeros((block, 128), jnp.float32)
-    acc = lax.fori_loop(0, quarter, functools.partial(propagate, False), acc)
-    acc = lax.fori_loop(quarter, 3 * quarter, functools.partial(propagate, True), acc)
-    acc = lax.fori_loop(3 * quarter, dirs, functools.partial(propagate, False), acc)
-    decay = jnp.exp(-0.5 * (sum_rows(acc) * scale))
-    decay = jnp.concatenate([decay] * (block // 8), axis=0)
-    grow = jnp.exp(wind_ref[...])
-    pick = jnp.where(iota((block, freqs), 0) // 2 == iota((block, freqs), 1), 1.0, 0.0)
-    grow = jnp.dot(
-        pick.astype(jnp.float32), grow, precision=HIGHEST, preferred_element_type=jnp.float32
-    )
-    turning = fields[1]
-
-    def finish(d, g):
-        before = jnp.where(d == 0, dirs - 1, d - 1)
-        after = jnp.where(d == dirs - 1, 0, d + 1)
-        p = prop[pl.ds(pl.multiple_of(d * block, 8), block)]
-        pb = prop[pl.ds(pl.multiple_of(before * block, 8), block)]
-        pa = prop[pl.ds(pl.multiple_of(after * block, 8), block)]
-        spread = p + turning * (pb + pa - 2.0 * p)
-        factor = jnp.broadcast_to(g[:, 0:1], (block, 128)) * decay
-        act_out[pl.ds(pl.multiple_of(d * block, 8), block)] = spread * factor
-        return pltpu.roll(g, 127, 1)
-
-    lax.fori_loop(0, dirs, finish, grow)
-
     own = sub // 4 == jnp.full((8, 128), own_half, jnp.int32)
     own1 = same(own_half, 1)
 
@@ -604,13 +682,13 @@
 
     lax.fori_loop(0, SUBSTEPS * GROUPS, drain_edges, 0)
 
-    @pl.when((core == 0) | has_outer)
-    def _():
-        flux_copy(0, core_id).wait_send()
-
-    @pl.when((core == 1) | has_outer)
-    def _():
-        flux_copy(1, core_id).wait_send()
+    for side in range(2):
+
+        @pl.when(flux_goes[side])
+        def _(side=side):
+            lax.fori_loop(
+                0, CHUNKS, lambda i, c: (flux_copy(side, i).wait_send(), c)[1], 0
+            )
 
 
 def halves(tile):
@@ -644,9 +722,9 @@
     rows = dirs * freqs * 2
     angles = (np.arange(dirs) + 0.5) * (2.0 * math.pi / dirs) - 0.5 * math.pi
     trig = jnp.asarray(np.abs(np.stack([np.cos(angles), np.sin(angles)])).astype(np.float32))
-    wind = jnp.pad(wind_growth.T, ((0, 0), (0, 128 - dirs)))
     vmem = pl.BlockSpec(memory_space=pltpu.VMEM)
-    smem = pl.BlockSpec(memory_space=pltpu.SMEM)
+    hbm = pl.BlockSpec(memory_space=pltpu.HBM)
+    S = pltpu.SMEM
     slots = SUBSTEPS * GROUPS
     f32 = jnp.float32
     V = pltpu.VMEM
@@ -656,7 +734,7 @@
             jax.ShapeDtypeStruct((classes, levels, 8, 128), f32),
             jax.ShapeDtypeStruct((rows, 128), f32),
         ),
-        in_specs=[vmem] * 5 + [smem] * 4 + [vmem, vmem, smem],
+        in_specs=[hbm] * 12,
         out_specs=(vmem, vmem),
         scratch_shapes=[
             V((GROUPS, 32 * 8, 128), f32),
@@ -679,14 +757,30 @@
             V((rows, 128), f32),
             V((rows, 128), f32),
             V((2, 2 * freqs, 128), f32),
+            V((2 * freqs, 128), f32),
+            V((2 * freqs, 128), f32),
+            V((2 * freqs, 128), f32),
+            V((classes, levels, 8, 128), f32),
+            V((2, 8, 128), f32),
+            V((8, 128), f32),
+            V((8, 128), jnp.int32),
+            V((levels, 8, 128), f32),
+            S((classes, classes), f32),
+            S((classes, classes), f32),
+            S((classes,), f32),
+            S((classes,), f32),
+            V((rows, 128), f32),
+            V((freqs, dirs), f32),
+            S((2, dirs), f32),
+            pltpu.SemaphoreType.DMA((12,)),
             pltpu.SemaphoreType.DMA((2, GROUPS)),
             pltpu.SemaphoreType.DMA((2, slots, 4)),
             pltpu.SemaphoreType.DMA((2, GROUPS)),
             pltpu.SemaphoreType.DMA((2, 3)),
-            pltpu.SemaphoreType.DMA((2, 2)),
+            pltpu.SemaphoreType.DMA((2, 2, CHUNKS)),
         ],
         compiler_params=pltpu.CompilerParams(
-            collective_id=0, has_side_effects=True, vmem_limit_bytes=32 * 1024 * 1024
+            collective_id=0, has_side_effects=True, vmem_limit_bytes=60 * 1024 * 1024
         ),
     )(
         halves(floc_conc),
@@ -699,7 +793,7 @@
         settling,
         erosion,
         action_density.reshape(rows, 128),
-        wind,
+        wind_growth.T,
         trig,
     )
     return unhalves(out_floc), out_act.reshape(action_density.shape)

time: 50.5 us -> 40.2 us (0.80)
  Pallas kernels: 42.9 us -> 36.6 us
  local copies, waits for them, and re-layouts: 6.54 us -> 2.73 us
    pallas_call x1, Pallas kernels: 42.9 us -> 36.6 us  [body(): pl.pallas_call(functools.partial(kernel, classes, levels, dirs, freqs, pa...]
    unnamed x24 -> x4, local copies, waits for them, and re-layouts: 5.81 us -> 2.73 us
    pad x1 -> x0, local copies, waits for them, and re-layouts: 0.73 us -> none  [body(): wind = jnp.pad(wind_growth.T, ((0, 0), (0, 128 - dirs)))]
where the time goes in v2:
time: 40.2 us; the launch traced here: 40 us
  Pallas kernels  36.6 us (91%)
  local copies, waits for them, and re-layouts  2.73 us (7%)
  between operations  0.65 us (2%)
    pallas_call x1, Pallas kernels, body(): pl.pallas_call(functools.partial(kernel, classes, levels, dirs, freqs, pa...  36.6 us
    unnamed x4, local copies, waits for them, and re-layouts  2.73 us

profile of v2, /device:TPU:0, one launch (start us, length us, event | category | flops | bytes accessed | tf_op | source)
XLA Modules:
  0.0 40.0 jit_solution(14184529400341460544)
XLA Ops:
  0.6 36.6 %shard_map.131 = (f32[15,8,8,128]{3,2,1,0:T(8,128)}, f32[1152,128]{1,0:T(8,128)}) custom-call(f32[15,8,8,128]{3,2,1,0:T(8,128)} %bitcast.35, f32[2,8,128]{2,1,0:T(8,128)} %bitcast.38, f32[8,128]{1,0:T(8,128)} %bitcast.40, s32[8,128]{1,0:T(8,128)} %bitcast.41, f32[8,8,128]{2,1,0:T(8,128)} %bitcast.37, f32[15,15]{1,0:T(8,128)} %agg_hbm.1, f32[15,15]{1,0:T(8,128)} %brk_hbm.1, ...), custom_call_target="tpu_custom_call" | custom-call | tf_op jit(solution)/shard_map/pallas_call | solution.py:731
  37.3 0.0 copy-start
  37.3 1.9 %copy.23 = f32[15,8,4,256]{3,2,1,0:T(4,128)} copy(f32[15,8,4,256]{3,2,1,0:T(4,128)} %bitcast.36) | data formatting | bytes 983040
  39.2 0.0 copy-done
  39.2 0.8 %copy.24 = f32[36,16,1,256]{3,2,1,0:T(1,128)} copy(f32[36,16,1,256]{3,2,1,0:T(1,128)S(1)} %bitcast.34) | data formatting | bytes 1179648
Async XLA Ops:
  37.3 1.9 %copy-start = (f32[1152,128]{1,0:T(8,128)S(1)}, f32[1152,128]{1,0:T(8,128)}, u32[]{:S(2)}) copy-start(f32[1152,128]{1,0:T(8,128)} %get-tuple-element.5) | copy-start | bytes 1769476

commit v3 on v2

--- a/solution.py
+++ b/solution.py
@@ -389,6 +389,12 @@
         rows = [conc[group, pl.ds(8 * u, 8)] for u in range(layers + 2)]
         row_send[slot, 0] = conc.at[group][pl.ds(7, 32, stride=8), :]
         row_send[slot, 1] = conc.at[group][pl.ds(0, 32, stride=8), :]
+        for here, copy in edges[:2]:
+
+            @pl.when(here)
+            def _(copy=copy):
+                copy(slot).start()
+
         right = jnp.zeros((8, 128), jnp.float32)
         left = jnp.zeros((8, 128), jnp.float32)
         for u, v in enumerate(rows):
@@ -396,14 +402,14 @@
             left = jnp.where(lane == u, roll(v, u, 1), left)
         col_send[slot, 0] = right
         col_send[slot, 1] = left
-        for here, copy in edges:
+        for here, copy in edges[2:]:
 
             @pl.when(here)
             def _(copy=copy):
                 copy(slot).start()
 
     def begin(group):
-        init_copy(group).wait_recv()
+        init_copy(group).wait()
         for k in range(classes):
             t0, t1 = unpack_pair(
                 floc_ref[k, levels - 1 - 2 * group],
@@ -528,6 +534,14 @@
 
                 propagate(part in (1, 2), part)
 
+        @pl.when(t >= CHUNKS)
+        def _():
+            for side in range(2):
+
+                @pl.when(flux_goes[side])
+                def _(side=side):
+                    flux_copy(side, t - CHUNKS).wait_send()
+
         @pl.when(t == CHUNKS + 4)
         def _():
             decay = jnp.exp(-0.5 * (sum_rows(wave_sum[...]) * scale))
@@ -557,6 +571,10 @@
             @pl.when(here)
             def _(copy=copy):
                 copy(t).wait_recv()
+
+            @pl.when(edges[side][0])
+            def _(copy=copy):
+                copy(t).wait_send()
 
         from_low = row_recv.at[t, 0]
         from_high = row_recv.at[t, 1]
@@ -665,30 +683,10 @@
     small_copy(2, pair_id).wait_send()
 
     def drain_groups(g, carry):
-        init_copy(g).wait_send()
         back_copy(g).wait_send()
         return carry
 
     lax.fori_loop(0, GROUPS, drain_groups, 0)
-
-    def drain_edges(t, carry):
-        for here, copy in edges:
-
-            @pl.when(here)
-            def _(copy=copy):
-                copy(t).wait_send()
-
-        return carry
-
-    lax.fori_loop(0, SUBSTEPS * GROUPS, drain_edges, 0)
-
-    for side in range(2):
-
-        @pl.when(flux_goes[side])
-        def _(side=side):
-            lax.fori_loop(
-                0, CHUNKS, lambda i, c: (flux_copy(side, i).wait_send(), c)[1], 0
-            )
 
 
 def halves(tile):
@@ -737,7 +735,7 @@
         in_specs=[hbm] * 12,
         out_specs=(vmem, vmem),
         scratch_shapes=[
-            V((GROUPS, 32 * 8, 128), f32),
+            V((GROUPS, 33 * 8, 128), f32),
             V((GROUPS, 2, 8, 128), f32),
             V((5, 8, 128), f32),
             V((8, 128), f32),

time: 40.2 us -> 39.8 us (0.990)
    pallas_call x1, Pallas kernels: 36.6 us -> 36.2 us  [body(): pl.pallas_call(functools.partial(kernel, classes, levels, dirs, freqs, pa...]
where the time goes in v3:
time: 39.8 us; the launch traced here: 39.6 us
  Pallas kernels  36.2 us (91%)
  local copies, waits for them, and re-layouts  2.73 us (7%)
  between operations  0.65 us (2%)
    pallas_call x1, Pallas kernels, body(): pl.pallas_call(functools.partial(kernel, classes, levels, dirs, freqs, pa...  36.2 us
    unnamed x4, local copies, waits for them, and re-layouts  2.73 us

profile of v3, /device:TPU:0, one launch (start us, length us, event | category | flops | bytes accessed | tf_op | source)
XLA Modules:
  0.0 39.6 jit_solution(10132776560738791660)
XLA Ops:
  0.6 36.2 %shard_map.131 = (f32[15,8,8,128]{3,2,1,0:T(8,128)}, f32[1152,128]{1,0:T(8,128)}) custom-call(f32[15,8,8,128]{3,2,1,0:T(8,128)} %bitcast.35, f32[2,8,128]{2,1,0:T(8,128)} %bitcast.38, f32[8,128]{1,0:T(8,128)} %bitcast.40, s32[8,128]{1,0:T(8,128)} %bitcast.41, f32[8,8,128]{2,1,0:T(8,128)} %bitcast.37, f32[15,15]{1,0:T(8,128)} %agg_hbm.1, f32[15,15]{1,0:T(8,128)} %brk_hbm.1, ...), custom_call_target="tpu_custom_call" | custom-call | tf_op jit(solution)/shard_map/pallas_call | solution.py:729
  36.9 0.0 copy-start
  36.9 1.9 %copy.23 = f32[15,8,4,256]{3,2,1,0:T(4,128)} copy(f32[15,8,4,256]{3,2,1,0:T(4,128)} %bitcast.36) | data formatting | bytes 983040
  38.8 0.0 copy-done
  38.8 0.8 %copy.24 = f32[36,16,1,256]{3,2,1,0:T(1,128)} copy(f32[36,16,1,256]{3,2,1,0:T(1,128)S(1)} %bitcast.34) | data formatting | bytes 1179648
Async XLA Ops:
  36.9 1.9 %copy-start = (f32[1152,128]{1,0:T(8,128)S(1)}, f32[1152,128]{1,0:T(8,128)}, u32[]{:S(2)}) copy-start(f32[1152,128]{1,0:T(8,128)} %get-tuple-element.5) | copy-start | bytes 1769476
